TPU v7x, 32 devices: a whole 2x2x4 slice. The times are simulated.
32 devices in a mesh: seg: 2 (over y), row: 4 (over z), col: 4 (over x, core).
Axes of the slice: x: 2, y: 2, z: 4, core: 2. Of those that a mesh axis runs over, the one named last changes fastest.
Arguments:
- ld_tiles: bfloat16 [40, 40, 256, 256], P(('seg', 'row'), 'col'), parts along dimension 0, may hold values from -0.03125 to 0.03125
- tile_lists: int32 [40, 40], P(('seg', 'row'), 'col'), parts along dimension 0, may hold values from 0 to 19, as said below
- live_counts: int32 [40], P(('seg', 'row')), parts along dimension 0, may hold values from 10 to 40, as said below
- typed_mask: int32 [10240], P(('seg', 'row')), parts along dimension 0, may hold values 0 or 1
- solution: float32 [512, 5120], P(('seg', 'col'), 'row'), parts along dimension 0, may hold values from -6 to 6
- residual: float32 [512, 5120], P(('seg', 'col'), 'row'), parts along dimension 0
- direction: float32 [512, 5120], P(('seg', 'col'), 'row'), parts along dimension 0, may hold values from -6 to 6
Outputs:
- solution_next: float32 [512, 5120], P(('seg', 'col'), 'row'), parts along dimension 0
- residual_next: float32 [512, 5120], P(('seg', 'col'), 'row'), parts along dimension 0
- direction_next: float32 [512, 5120], P(('seg', 'col'), 'row'), parts along dimension 0
- imputed: float32 [512, 5120], P(('seg', 'col'), 'row'), parts along dimension 0
There are 2 independent parts, one for each index of `seg`. A program takes and returns all parts, laid end to end along the dimension named above; each array names one. Nothing has to cross between parts.
Inputs may be any that keep to these rules, and one draw needn't show every extreme that they name: `tile_lists`: slot s of tile row t names t + o - 20 clipped to 0 .. 19, where the offsets o of a row are a permutation of 0 .. 39. `live_counts`: some tile row has all 40 slots live and another has 10.
All inputs are finite; a program needn't handle non-finite values. No bound on the sum of `typed_mask` on one device may be relied on, other than what follows from the above.
Results may differ from a plain program's by a relative error of at most 0.0029.
Values may be sent and summed in bfloat16 or wider, within the bound.
No kernel may reach another device: no remote copies, remote signals or barrier semaphores. Data moves between devices by JAX's collectives and lax.ppermute only.
A program may use at most 64 MiB of HBM per device.

v0:
```python
import jax
import jax.numpy as jnp
from jax import lax
from jax.sharding import PartitionSpec as P

W = 40


def from_behind(block, axis, distance):
    devices = range(lax.axis_size(axis))
    route = [(i - distance, i) for i in devices if i - distance in devices]
    return lax.ppermute(block, axis, route)


def window_product(vectors, ld_tiles, tile_lists, live_counts):
    traits = vectors.shape[0]
    tile_rows = ld_tiles.shape[0]
    slot_count = ld_tiles.shape[1]
    tile_size = ld_tiles.shape[2]
    extent = min((W // 2 + tile_rows - 1) // tile_rows, lax.axis_size("row") - 1)
    pieces = [
        vectors if offset == 0 else from_behind(vectors, "row", -offset)
        for offset in range(-extent, extent + 1)
    ]
    window = jnp.concatenate(pieces, axis=1)
    lowest = (lax.axis_index("row") - extent) * tile_rows
    blocks = window.reshape(traits, window.shape[1] // tile_size, tile_size)
    position = (tile_lists - lowest).reshape(-1)
    picked = jnp.take(blocks, position, axis=1).reshape(traits, tile_rows, slot_count, tile_size)
    slot_index = lax.axis_index("col") * slot_count + jnp.arange(slot_count, dtype=jnp.int32)
    active = (slot_index[None, :] < live_counts[:, None]).astype(jnp.bfloat16)
    picked = picked * active[None, :, :, None]
    product = jnp.einsum("ktsj,tsij->kti", picked, ld_tiles, preferred_element_type=jnp.float32)
    return product.reshape(traits, tile_rows * tile_size)


def local(ld_tiles, tile_lists, live_counts, typed_mask, solution, residual, direction):
    typed_rows = typed_mask.astype(jnp.float32)[None, :]
    masked = (direction * typed_rows).astype(jnp.bfloat16)
    gathered = lax.all_gather(masked, "col", axis=0, tiled=True)
    partial_value = window_product(gathered, ld_tiles, tile_lists, live_counts)
    spread = lax.psum_scatter(partial_value, "col", scatter_dimension=0, tiled=True)
    search, current, remain = (direction, solution, residual)
    image = typed_rows * search + typed_rows * spread + 0.1 * search
    before, curve = lax.psum(
        (jnp.sum(remain * remain, axis=1), jnp.sum(search * image, axis=1)), "row"
    )
    alpha = (before / curve)[:, None]
    solution_next = current + alpha * search
    residual_next = remain - alpha * image
    after = lax.psum(jnp.sum(residual_next * residual_next, axis=1), "row")
    direction_next = residual_next + (after / before)[:, None] * search
    weights = (solution_next * typed_rows).astype(jnp.bfloat16)
    weights_all = lax.all_gather(weights, "col", axis=0, tiled=True)
    second = window_product(weights_all, ld_tiles, tile_lists, live_counts)
    summed = lax.psum_scatter(second, "col", scatter_dimension=0, tiled=True)
    imputed = (1.0 - typed_rows) * summed
    return (solution_next, residual_next, direction_next, imputed)


def solution(mesh):
    in_specs = (
        P(("seg", "row"), "col", None, None),
        P(("seg", "row"), "col"),
        P(("seg", "row")),
        P(("seg", "row")),
        P(("seg", "col"), "row"),
        P(("seg", "col"), "row"),
        P(("seg", "col"), "row"),
    )
    out_specs = (
        P(("seg", "col"), "row"),
        P(("seg", "col"), "row"),
        P(("seg", "col"), "row"),
        P(("seg", "col"), "row"),
    )
    return jax.shard_map(local, mesh=mesh, in_specs=in_specs, out_specs=out_specs, check_vma=False)
```

profile of v0, /device:TPU:12, one launch (start us, length us, event | category | flops | bytes accessed | tf_op | source)
XLA Modules:
  0.0 283.4 jit_solution(7615249967108556515)
XLA Ops:
  7.9 1.0 multiply_convert_fusion.1
  8.9 7.9 %all_gather.6 = bf16[256,1280]{1,0:T(8,128)(2,1)S(1)} all-gather(bf16[64,1280]{1,0:T(8,128)(2,1)S(1)} %multiply_convert_fusion.1), channel_id=1, replica_groups=mesh['seg'=2,'row'=4,'col'=4] {'col'}, dimensions={0}, use_global_device_ids=true | all-gather | bytes 819200 | tf_op jit(solution)/shard_map/all_gather | solution.py:40
  17.0 1.5 collective-permute-start
  18.6 4.3 %collective-permute-start.1 = (bf16[256,1280]{0,1:T(8,128)(2,1)S(1)}, bf16[256,1280]{0,1:T(8,128)(2,1)S(1)}, u32[]{:S(2)}, u32[]{:S(2)}) collective-permute-start(bf16[256,1280]{0,1:T(8,128)(2,1)S(1)} %copy.28), channel_id=1, source_target_pairs={{0,8},{4,12},{1,9},{5,13},{2,10},{6,14},{3,11},{7,15},{16,24},{20,... | collective-permute-start | bytes 1966088 | tf_op jit(solution)/shard_map/ppermute | solution.py:12
  22.9 1.9 collective-permute-start.2
  24.8 4.0 %collective-permute-start.3 = (bf16[256,1280]{0,1:T(8,128)(2,1)S(1)}, bf16[256,1280]{0,1:T(8,128)(2,1)S(1)}, u32[]{:S(2)}, u32[]{:S(2)}) collective-permute-start(bf16[256,1280]{0,1:T(8,128)(2,1)S(1)} %copy.28), channel_id=1, source_target_pairs={{4,0},{8,4},{12,8},{5,1},{9,5},{13,9},{6,2},{10,6},{14,10},{7,3},{... | collective-permute-start | bytes 1966088 | tf_op jit(solution)/shard_map/ppermute | solution.py:12
  28.8 1.3 collective-permute-start.4
  32.3 2.0 constant_dynamic-update-slice_fusion.6
  34.3 30.8 %collective-permute-done.1 = bf16[256,1280]{0,1:T(8,128)(2,1)S(1)} collective-permute-done((bf16[256,1280]{0,1:T(8,128)(2,1)S(1)}, bf16[256,1280]{0,1:T(8,128)(2,1)S(1)}, u32[]{:S(2)}, u32[]{:S(2)}) %collective-permute-start.1) | collective-permute-done | bytes 655392 | tf_op jit(solution)/shard_map/ppermute | solution.py:12
  65.1 0.9 constant_dynamic-update-slice_fusion.5
  66.0 13.1 %collective-permute-done.2 = bf16[256,1280]{0,1:T(8,128)(2,1)S(1)} collective-permute-done((bf16[256,1280]{0,1:T(8,128)(2,1)S(1)}, bf16[256,1280]{0,1:T(8,128)(2,1)S(1)}, u32[]{:S(2)}, u32[]{:S(2)}) %collective-permute-start.2) | collective-permute-done | bytes 655392 | tf_op jit(solution)/shard_map/ppermute | solution.py:12
  79.1 0.9 constant_dynamic-update-slice_fusion.4
  80.0 0.9 constant_dynamic-update-slice_fusion.3
  80.9 0.9 constant_dynamic-update-slice_fusion.2
  81.8 0.9 constant_dynamic-update-slice_fusion.1
  82.7 0.9 constant_dynamic-update-slice_fusion
  83.6 6.6 %copy.35 = bf16[256,35,256]{2,0,1:T(8,128)(2,1)} copy(bf16[256,35,256]{0,2,1:T(8,128)(2,1)} %bitcast) | data formatting | bytes 9175040 | tf_op jit(solution)/shard_map/reshape | solution.py:27
  90.2 7.3 %gather_fusion = bf16[50,256,256]{2,1,0:T(8,128)(2,1)} fusion(bf16[256,35,256]{2,0,1:T(8,128)(2,1)} %copy.35, s32[1024]{0:T(1024)S(1)} %pad_clamp_fusion), kind=kCustom, calls=%fused_computation.clone | custom fusion | bytes 13107400 | tf_op jit(solution)/shard_map/jit(_take)/gather | solution.py:29
  97.5 3.5 %broadcast_select_fusion.1 = bf16[50,256,256]{2,1,0:T(8,128)(2,1)S(1)} fusion(bf16[50,256,256]{2,1,0:T(8,128)(2,1)} %gather_fusion, pred[50]{0:T(512)(128)(4,1)S(1)} %compare_and_fusion), kind=kLoop, calls=%fused_computation.7 | loop fusion | flops 3276800 | bytes 13107250 | tf_op jit(solution)/shard_map/jit(_take)/select_n | solution.py:29
  101.1 4.9 %fusion.2 = f32[5,256,256,1]{1,2,3,0:T(8,128)S(1)} fusion(bf16[5,10,256,256]{3,2,1,0:T(8,128)(2,1)} %param.9, bf16[256,5,10,256]{3,0,2,1:T(8,128)(2,1)S(1)} %bitcast.24, bf16[5,10]{1,0:T(8,128)(2,1)S(1)} %compare_convert_fusion), kind=kOutput, calls=%fused_computation.4 | convolution fusion | flops 1680998400 | bytes 14418020 | tf_op jit(solution)/shard_map/ktsj,tsij->kti/dot_general | solution.py:33
  106.0 1.5 copy.48
  107.7 29.0 %reduce-scatter.7.cloned.1.call-done = f32[64,1280]{1,0:T(8,128)} async-done(((f32[256,1280]{1,0:T(8,128)}), f32[64,1280]{1,0:T(8,128)}) %reduce-scatter.7.cloned.1.call-update) | async-done | bytes 327696 | tf_op jit(solution)/shard_map/reduce_scatter | solution.py:42
  136.7 1.1 multiply_reduce_fusion.1
  137.8 8.9 %all-reduce = (f32[64]{0:T(128)S(1)}, f32[64]{0:T(128)S(1)}) all-reduce(f32[64]{0:T(128)S(1)} %multiply_reduce_fusion.2, f32[64]{0:T(128)S(1)} %multiply_reduce_fusion.1), channel_id=1, replica_groups=mesh['seg'=2,'row'=4,'col'=4] {'row'}, use_global_device_ids=true, to_apply=%region_1.2 | all-reduce | flops 128 | bytes 1024 | tf_op jit(solution)/shard_map/psum | solution.py:45
  146.7 2.0 multiply_reduce_fusion
  148.7 7.0 %all_gather.7 = bf16[256,1280]{1,0:T(8,128)(2,1)S(1)} all-gather(bf16[64,1280]{1,0:T(8,128)(2,1)S(1)} %get-tuple-element.15), channel_id=1, replica_groups=mesh['seg'=2,'row'=4,'col'=4] {'col'}, dimensions={0}, use_global_device_ids=true | all-gather | bytes 819200 | tf_op jit(solution)/shard_map/all_gather | solution.py:54
  156.6 4.2 %collective-permute-start.7 = (bf16[256,1280]{0,1:T(8,128)(2,1)S(1)}, bf16[256,1280]{0,1:T(8,128)(2,1)S(1)}, u32[]{:S(2)}, u32[]{:S(2)}) collective-permute-start(bf16[256,1280]{0,1:T(8,128)(2,1)S(1)} %copy.37), channel_id=1, source_target_pairs={{0,8},{4,12},{1,9},{5,13},{2,10},{6,14},{3,11},{7,15},{16,24},{20,... | collective-permute-start | bytes 1966088 | tf_op jit(solution)/shard_map/ppermute | solution.py:12
  160.8 1.9 collective-permute-start.8
  162.7 4.0 %collective-permute-start.9 = (bf16[256,1280]{0,1:T(8,128)(2,1)S(1)}, bf16[256,1280]{0,1:T(8,128)(2,1)S(1)}, u32[]{:S(2)}, u32[]{:S(2)}) collective-permute-start(bf16[256,1280]{0,1:T(8,128)(2,1)S(1)} %copy.37), channel_id=1, source_target_pairs={{4,0},{8,4},{12,8},{5,1},{9,5},{13,9},{6,2},{10,6},{14,10},{7,3},{... | collective-permute-start | bytes 1966088 | tf_op jit(solution)/shard_map/ppermute | solution.py:12
  166.7 1.3 collective-permute-start.10
  168.0 0.9 collective-permute-start.11
  168.9 0.9 constant_dynamic-update-slice_fusion.13
  169.8 33.2 %collective-permute-done.7 = bf16[256,1280]{0,1:T(8,128)(2,1)S(1)} collective-permute-done((bf16[256,1280]{0,1:T(8,128)(2,1)S(1)}, bf16[256,1280]{0,1:T(8,128)(2,1)S(1)}, u32[]{:S(2)}, u32[]{:S(2)}) %collective-permute-start.7) | collective-permute-done | bytes 655392 | tf_op jit(solution)/shard_map/ppermute | solution.py:12
  203.0 0.9 constant_dynamic-update-slice_fusion.12
  203.9 13.1 %collective-permute-done.8 = bf16[256,1280]{0,1:T(8,128)(2,1)S(1)} collective-permute-done((bf16[256,1280]{0,1:T(8,128)(2,1)S(1)}, bf16[256,1280]{0,1:T(8,128)(2,1)S(1)}, u32[]{:S(2)}, u32[]{:S(2)}) %collective-permute-start.8) | collective-permute-done | bytes 655392 | tf_op jit(solution)/shard_map/ppermute | solution.py:12
  217.0 0.9 constant_dynamic-update-slice_fusion.11
  217.9 0.9 constant_dynamic-update-slice_fusion.10
  218.8 0.9 constant_dynamic-update-slice_fusion.9
  219.7 0.9 constant_dynamic-update-slice_fusion.8
  220.6 0.9 constant_dynamic-update-slice_fusion.7
  221.5 6.6 %copy.44 = bf16[256,35,256]{2,0,1:T(8,128)(2,1)} copy(bf16[256,35,256]{0,2,1:T(8,128)(2,1)} %bitcast.7) | data formatting | bytes 9175040 | tf_op jit(solution)/shard_map/reshape | solution.py:27
  228.1 7.3 %gather_fusion.1 = bf16[50,256,256]{2,1,0:T(8,128)(2,1)} fusion(bf16[256,35,256]{2,0,1:T(8,128)(2,1)} %copy.44, s32[1024]{0:T(1024)S(1)} %pad_clamp_fusion), kind=kCustom, calls=%fused_computation.1.clone | custom fusion | bytes 13107400 | tf_op jit(solution)/shard_map/jit(_take)/gather | solution.py:29
  235.4 3.5 %broadcast_select_fusion = bf16[50,256,256]{2,1,0:T(8,128)(2,1)S(1)} fusion(bf16[50,256,256]{2,1,0:T(8,128)(2,1)} %gather_fusion.1, pred[50]{0:T(512)(128)(4,1)S(1)} %compare_and_fusion), kind=kLoop, calls=%fused_computation.6 | loop fusion | flops 3276800 | bytes 13107250 | tf_op jit(solution)/shard_map/jit(_take)/select_n | solution.py:29
  239.0 4.9 %fusion = f32[5,256,256,1]{1,2,3,0:T(8,128)S(1)} fusion(bf16[5,10,256,256]{3,2,1,0:T(8,128)(2,1)} %param.9, bf16[256,5,10,256]{3,0,2,1:T(8,128)(2,1)S(1)} %bitcast.23, bf16[5,10]{1,0:T(8,128)(2,1)S(1)} %compare_convert_fusion), kind=kOutput, calls=%fused_computation.2 | convolution fusion | flops 1680998400 | bytes 14418020 | tf_op jit(solution)/shard_map/ktsj,tsij->kti/dot_general | solution.py:33
  243.9 1.5 copy.45
  245.4 13.5 %psum.23 = f32[64]{0:T(128)S(1)} all-reduce(f32[64]{0:T(128)S(1)} %get-tuple-element.13), channel_id=1, replica_groups=mesh['seg'=2,'row'=4,'col'=4] {'row'}, use_global_device_ids=true, to_apply=%region_6.8 | all-reduce | flops 64 | bytes 512 | tf_op jit(solution)/shard_map/psum | solution.py:51
  259.7 15.1 %reduce-scatter.5.cloned.1.call-done = f32[64,1280]{1,0:T(8,128)} async-done(((f32[256,1280]{1,0:T(8,128)}), f32[64,1280]{1,0:T(8,128)}) %reduce-scatter.5.cloned.1.call-update) | async-done | bytes 327696 | tf_op jit(solution)/shard_map/reduce_scatter | solution.py:56
  274.9 1.7 broadcast_multiply_fusion
  (39 shorter events, 5.2 us)
Async XLA Ops:
  7.2 129.5 %reduce-scatter.7.cloned.1.call-start = ((), (), s32[]{:S(2)}) async-start(), calls=%async_computation.3 | async-start | bytes 1638400 | tf_op jit(solution)/shard_map/reduce_scatter | solution.py:42
  17.0 14.6 %collective-permute-start = (bf16[256,1280]{0,1:T(8,128)(2,1)S(1)}, bf16[256,1280]{0,1:T(8,128)(2,1)}, u32[]{:S(2)}, u32[]{:S(2)}) collective-permute-start(bf16[256,1280]{0,1:T(8,128)(2,1)S(1)} %copy.28), channel_id=1, source_target_pairs={{0,12},{1,13},{2,14},{3,15},{16,28},{17,29},{18,30},{19,31}} | collective-permute-start | bytes 1966088 | tf_op jit(solution)/shard_map/ppermute | solution.py:12
  18.6 46.5 %collective-permute-start.1 = (bf16[256,1280]{0,1:T(8,128)(2,1)S(1)}, bf16[256,1280]{0,1:T(8,128)(2,1)S(1)}, u32[]{:S(2)}, u32[]{:S(2)}) collective-permute-start(bf16[256,1280]{0,1:T(8,128)(2,1)S(1)} %copy.28), channel_id=1, source_target_pairs={{0,8},{4,12},{1,9},{5,13},{2,10},{6,14},{3,11},{7,15},{16,24},{20,... | collective-permute-start | bytes 1966088 | tf_op jit(solution)/shard_map/ppermute | solution.py:12
  22.9 56.2 %collective-permute-start.2 = (bf16[256,1280]{0,1:T(8,128)(2,1)S(1)}, bf16[256,1280]{0,1:T(8,128)(2,1)S(1)}, u32[]{:S(2)}, u32[]{:S(2)}) collective-permute-start(bf16[256,1280]{0,1:T(8,128)(2,1)S(1)} %copy.28), channel_id=1, source_target_pairs={{0,4},{4,8},{8,12},{1,5},{5,9},{9,13},{2,6},{6,10},{10,14},{3,7},{... | collective-permute-start | bytes 1966088 | tf_op jit(solution)/shard_map/ppermute | solution.py:12
  24.8 56.1 %collective-permute-start.3 = (bf16[256,1280]{0,1:T(8,128)(2,1)S(1)}, bf16[256,1280]{0,1:T(8,128)(2,1)S(1)}, u32[]{:S(2)}, u32[]{:S(2)}) collective-permute-start(bf16[256,1280]{0,1:T(8,128)(2,1)S(1)} %copy.28), channel_id=1, source_target_pairs={{4,0},{8,4},{12,8},{5,1},{9,5},{13,9},{6,2},{10,6},{14,10},{7,3},{... | collective-permute-start | bytes 1966088 | tf_op jit(solution)/shard_map/ppermute | solution.py:12
  28.8 53.0 %collective-permute-start.4 = (bf16[256,1280]{0,1:T(8,128)(2,1)S(1)}, bf16[256,1280]{0,1:T(8,128)(2,1)S(1)}, u32[]{:S(2)}, u32[]{:S(2)}) collective-permute-start(bf16[256,1280]{0,1:T(8,128)(2,1)S(1)} %copy.28), channel_id=1, source_target_pairs={{8,0},{12,4},{9,1},{13,5},{10,2},{14,6},{11,3},{15,7},{24,16},{28,... | collective-permute-start | bytes 1966088 | tf_op jit(solution)/shard_map/ppermute | solution.py:12
  31.6 51.0 %collective-permute-start.5 = (bf16[256,1280]{0,1:T(8,128)(2,1)S(1)}, bf16[256,1280]{0,1:T(8,128)(2,1)S(1)}, u32[]{:S(2)}, u32[]{:S(2)}) collective-permute-start(bf16[256,1280]{0,1:T(8,128)(2,1)S(1)} %copy.28), channel_id=1, source_target_pairs={{12,0},{13,1},{14,2},{15,3},{28,16},{29,17},{30,18},{31,19}} | collective-permute-start | bytes 1966088 | tf_op jit(solution)/shard_map/ppermute | solution.py:12
  101.0 6.5 %copy-start.2 = (f32[64,1280]{1,0:T(8,128)S(1)}, f32[64,1280]{1,0:T(8,128)}, u32[]{:S(2)}) copy-start(f32[64,1280]{1,0:T(8,128)} %param.14) | copy-start | bytes 983044
  101.1 35.6 %copy-start = (f32[64,1280]{1,0:T(8,128)S(1)}, f32[64,1280]{1,0:T(8,128)}, u32[]{:S(2)}) copy-start(f32[64,1280]{1,0:T(8,128)} %param.15) | copy-start | bytes 983044
  106.0 40.7 %copy-start.3 = (f32[64,1280]{1,0:T(8,128)S(1)}, f32[64,1280]{1,0:T(8,128)}, u32[]{:S(2)}) copy-start(f32[64,1280]{1,0:T(8,128)} %param.13) | copy-start | bytes 983044
  107.5 167.4 %reduce-scatter.5.cloned.1.call-start = ((), (), s32[]{:S(2)}) async-start(), calls=%async_computation.2 | async-start | bytes 1638400 | tf_op jit(solution)/shard_map/reduce_scatter | solution.py:56
  148.7 110.2 %copy-start.1 = (f32[64,1280]{1,0:T(8,128)}, f32[64,1280]{1,0:T(8,128)S(1)}, u32[]{:S(2)}) copy-start(f32[64,1280]{1,0:T(8,128)S(1)} %get-tuple-element.14) | copy-start | bytes 983044
  155.9 12.1 %collective-permute-start.6 = (bf16[256,1280]{0,1:T(8,128)(2,1)S(1)}, bf16[256,1280]{0,1:T(8,128)(2,1)S(1)}, u32[]{:S(2)}, u32[]{:S(2)}) collective-permute-start(bf16[256,1280]{0,1:T(8,128)(2,1)S(1)} %copy.37), channel_id=1, source_target_pairs={{0,12},{1,13},{2,14},{3,15},{16,28},{17,29},{18,30},{19,31}} | collective-permute-start | bytes 1966088 | tf_op jit(solution)/shard_map/ppermute | solution.py:12
  156.6 46.4 %collective-permute-start.7 = (bf16[256,1280]{0,1:T(8,128)(2,1)S(1)}, bf16[256,1280]{0,1:T(8,128)(2,1)S(1)}, u32[]{:S(2)}, u32[]{:S(2)}) collective-permute-start(bf16[256,1280]{0,1:T(8,128)(2,1)S(1)} %copy.37), channel_id=1, source_target_pairs={{0,8},{4,12},{1,9},{5,13},{2,10},{6,14},{3,11},{7,15},{16,24},{20,... | collective-permute-start | bytes 1966088 | tf_op jit(solution)/shard_map/ppermute | solution.py:12
  160.8 56.2 %collective-permute-start.8 = (bf16[256,1280]{0,1:T(8,128)(2,1)S(1)}, bf16[256,1280]{0,1:T(8,128)(2,1)S(1)}, u32[]{:S(2)}, u32[]{:S(2)}) collective-permute-start(bf16[256,1280]{0,1:T(8,128)(2,1)S(1)} %copy.37), channel_id=1, source_target_pairs={{0,4},{4,8},{8,12},{1,5},{5,9},{9,13},{2,6},{6,10},{10,14},{3,7},{... | collective-permute-start | bytes 1966088 | tf_op jit(solution)/shard_map/ppermute | solution.py:12
  162.7 56.1 %collective-permute-start.9 = (bf16[256,1280]{0,1:T(8,128)(2,1)S(1)}, bf16[256,1280]{0,1:T(8,128)(2,1)S(1)}, u32[]{:S(2)}, u32[]{:S(2)}) collective-permute-start(bf16[256,1280]{0,1:T(8,128)(2,1)S(1)} %copy.37), channel_id=1, source_target_pairs={{4,0},{8,4},{12,8},{5,1},{9,5},{13,9},{6,2},{10,6},{14,10},{7,3},{... | collective-permute-start | bytes 1966088 | tf_op jit(solution)/shard_map/ppermute | solution.py:12
  166.7 53.0 %collective-permute-start.10 = (bf16[256,1280]{0,1:T(8,128)(2,1)S(1)}, bf16[256,1280]{0,1:T(8,128)(2,1)S(1)}, u32[]{:S(2)}, u32[]{:S(2)}) collective-permute-start(bf16[256,1280]{0,1:T(8,128)(2,1)S(1)} %copy.37), channel_id=1, source_target_pairs={{8,0},{12,4},{9,1},{13,5},{10,2},{14,6},{11,3},{15,7},{24,16},{28,... | collective-permute-start | bytes 1966088 | tf_op jit(solution)/shard_map/ppermute | solution.py:12
  168.0 52.6 %collective-permute-start.11 = (bf16[256,1280]{0,1:T(8,128)(2,1)S(1)}, bf16[256,1280]{0,1:T(8,128)(2,1)S(1)}, u32[]{:S(2)}, u32[]{:S(2)}) collective-permute-start(bf16[256,1280]{0,1:T(8,128)(2,1)S(1)} %copy.37), channel_id=1, source_target_pairs={{12,0},{13,1},{14,2},{15,3},{28,16},{29,17},{30,18},{31,19}} | collective-permute-start | bytes 1966088 | tf_op jit(solution)/shard_map/ppermute | solution.py:12
  239.0 6.4 %copy-start.4 = (s32[1280]{0:T(1024)S(1)}, s32[1280]{0:T(1024)}, u32[]{:S(2)}) copy-start(s32[1280]{0:T(1024)} %param.12) | copy-start | bytes 15364
Sparse Core Ops, SparseCore 0:
  107.7 28.9 reduce-scatter.6
  245.5 29.3 reduce-scatter.4
where the time goes:
time: 286 us; the launch traced here: 283 us
  waiting for transfers between devices  134 us (47%)
  local copies, waits for them, and re-layouts  44.9 us (16%)
  blocking collectives  37.3 us (13%)
  starting transfers between devices  26.7 us (9%)
  other arithmetic  16 us (6%)
  between operations  14.3 us (5%)
  matrix products  9.82 us (3%)
    ppermute x12, waiting for transfers between devices, from_behind(): return lax.ppermute(block, axis, route)  90.3 us
    reduce_scatter x1, waiting for transfers between devices, local(): lax.psum_scatter(partial_value, 'col', scatter_dimension=0, tiled=True)  29 us
    ppermute x12, starting transfers between devices, from_behind(): return lax.ppermute(block, axis, route)  26.6 us
    reduce_scatter x1, waiting for transfers between devices, local(): summed = lax.psum_scatter(second, 'col', scatter_dimension=0, tiled=True)  15.1 us
    gather x2, local copies, waits for them, and re-layouts, window_product(): jnp.take(blocks, position, axis=1)  14.6 us
    psum x1, blocking collectives, local(): after = lax.psum(jnp.sum(residual_next * residual_next, axis=1), 'row')  13.5 us
    reshape x2, local copies, waits for them, and re-layouts, window_product(): blocks = window.reshape(traits, window.shape[1] // tile_size, tile_size)  13.2 us
    unnamed x23, local copies, waits for them, and re-layouts  13.2 us
  transfers between devices with their start and end apart: 14, of which 6 were waited for; matrix products, arithmetic and copies ran while one was open for 5% of the time, Pallas kernels for 0%

commit v1 on v0

v1 whole, which is shorter than its diff:
```python
import functools

import jax
import jax.numpy as jnp
from jax import lax
from jax.experimental import pallas as pl
from jax.experimental.pallas import tpu as pltpu
from jax.sharding import PartitionSpec as P

W = 40


def from_behind(block, axis, distance):
    devices = range(lax.axis_size(axis))
    route = [(i - distance, i) for i in devices if i - distance in devices]
    return lax.ppermute(block, axis, route)


def gather_window(block, extent):
    rows, cols = lax.axis_size("row"), lax.axis_size("col")
    if extent >= rows - 1:
        whole = lax.all_gather(block, ("row", "col"), axis=0, tiled=False)
        return whole.reshape((rows, cols) + block.shape)
    mine = lax.all_gather(block, "col", axis=0, tiled=False)
    pieces = [
        mine if offset == 0 else from_behind(mine, "row", -offset)
        for offset in range(-extent, extent + 1)
    ]
    return jnp.stack(pieces)


def product_kernel(tile_rows, slots, tile_size, place_ref, live_ref, v_ref, ld_ref, out_ref):
    t = pl.program_id(0)
    cols, depth = v_ref.shape[1], v_ref.shape[2]
    traits = cols * depth

    def one_slot(s, total):
        place = place_ref[t, s]
        piece = place // tile_rows
        start = pl.multiple_of((place - piece * tile_rows) * tile_size, tile_size)
        picked = v_ref[piece, :, :, pl.ds(start, tile_size)].reshape(traits, tile_size)
        return total + lax.dot_general(
            picked, ld_ref[0, s], (((1,), (1,)), ((), ())),
            preferred_element_type=jnp.float32,
        )

    total = lax.fori_loop(
        0, live_ref[t], one_slot, jnp.zeros((traits, tile_size), jnp.float32)
    )
    out_ref[...] = total.reshape(cols, depth, tile_size)


def window_product(vectors, ld_tiles, place, live):
    tile_rows, slots, tile_size, _ = ld_tiles.shape
    pieces, cols, depth, width = vectors.shape
    return pl.pallas_call(
        functools.partial(product_kernel, tile_rows, slots, tile_size),
        grid=(tile_rows,),
        in_specs=[
            pl.BlockSpec(memory_space=pltpu.SMEM),
            pl.BlockSpec(memory_space=pltpu.SMEM),
            pl.BlockSpec((pieces, cols, depth, width), lambda t: (0, 0, 0, 0)),
            pl.BlockSpec((1, slots, tile_size, tile_size), lambda t: (t, 0, 0, 0)),
        ],
        out_specs=pl.BlockSpec((cols, depth, tile_size), lambda t: (0, 0, t)),
        out_shape=jax.ShapeDtypeStruct((cols, depth, tile_rows * tile_size), jnp.float32),
        compiler_params=pltpu.CompilerParams(vmem_limit_bytes=40 * 1024 * 1024),
        cost_estimate=pl.CostEstimate(
            flops=2 * cols * depth * tile_rows * slots * tile_size**2,
            bytes_accessed=2 * ld_tiles.size + 2 * vectors.size + 4 * cols * depth * width,
            transcendentals=0,
        ),
        name="window_product",
    )(place, live, vectors, ld_tiles)


def local(ld_tiles, tile_lists, live_counts, typed_mask, solution, residual, direction):
    tile_rows, slots = tile_lists.shape
    extent = min((W // 2 + tile_rows - 1) // tile_rows, lax.axis_size("row") - 1)
    lowest = lax.axis_index("row") - extent
    if extent >= lax.axis_size("row") - 1:
        lowest = 0
    place = tile_lists - lowest * tile_rows
    live = jnp.clip(live_counts - lax.axis_index("col") * slots, 0, slots)

    typed = typed_mask.astype(jnp.float32)[None, :]
    masked = (direction * typed).astype(jnp.bfloat16)
    known = (solution * typed).astype(jnp.bfloat16)
    masked_all = gather_window(masked, extent)
    known_all = gather_window(known, extent)
    spread = lax.psum_scatter(
        window_product(masked_all, ld_tiles, place, live), "col", scatter_dimension=0
    )
    image = typed * direction + typed * spread + 0.1 * direction
    before, curve, cross, square = lax.psum(
        jnp.stack([
            jnp.sum(residual * residual, axis=1),
            jnp.sum(direction * image, axis=1),
            jnp.sum(residual * image, axis=1),
            jnp.sum(image * image, axis=1),
        ]),
        "row",
    )
    alpha = before / curve
    after = before + alpha * (alpha * square - 2.0 * cross)
    beta = after / before
    alpha, beta = alpha[:, None], beta[:, None]
    solution_next = solution + alpha * direction
    residual_next = residual - alpha * image
    direction_next = residual_next + beta * direction
    held = lax.psum_scatter(
        window_product(known_all, ld_tiles, place, live), "col", scatter_dimension=0
    )
    imputed = (1.0 - typed) * (held + alpha * spread)
    return (solution_next, residual_next, direction_next, imputed)


def solution(mesh):
    in_specs = (
        P(("seg", "row"), "col", None, None),
        P(("seg", "row"), "col"),
        P(("seg", "row")),
        P(("seg", "row")),
        P(("seg", "col"), "row"),
        P(("seg", "col"), "row"),
        P(("seg", "col"), "row"),
    )
    out_specs = (P(("seg", "col"), "row"),) * 4
    return jax.shard_map(local, mesh=mesh, in_specs=in_specs, out_specs=out_specs, check_vma=False)
```

time: 286 us -> 208 us (0.73)
  local copies, waits for them, and re-layouts: 44.9 us -> 9.91 us
  blocking collectives: 37.3 us -> 8.9 us
  Pallas kernels: 0 us -> 26.8 us
  starting transfers between devices: 26.7 us -> 0.16 us
  matrix products: 9.82 us -> 0 us
  other arithmetic: 16 us -> 7.22 us
  waiting for transfers between devices: 134 us -> 139 us
    ppermute x12 -> x0, waiting for transfers between devices: 90.3 us -> none  [from_behind(): return lax.ppermute(block, axis, route)]
    all_gather x0 -> x2, waiting for transfers between devices: none -> 87.8 us  [gather_window(): whole = lax.all_gather(block, ('row', 'col'), axis=0, tiled=False)]
    pallas_call x0 -> x2, Pallas kernels: none -> 26.8 us  [window_product(): pl.pallas_call(functools.partial(product_kernel, tile_rows, slots, tile_s...]
    ppermute x12 -> x0, starting transfers between devices: 26.6 us -> none  [from_behind(): return lax.ppermute(block, axis, route)]
    all_gather x2 -> x0, blocking collectives: 14.8 us -> none  [the longest x1 7.89 us: local(): gathered = lax.all_gather(masked, 'col', axis=0, tiled=True)]
    reshape x4 -> x0, local copies, waits for them, and re-layouts: 14.8 us -> none  [the longest x2 13.2 us: window_product(): blocks = window.reshape(traits, window.shape[1] // tile_size, tile_size)]
    gather x2 -> x0, local copies, waits for them, and re-layouts: 14.6 us -> none  [window_product(): jnp.take(blocks, position, axis=1)]
    psum x2 -> x1, blocking collectives: 22.4 us -> 8.9 us  [local(): lax.psum(jnp.stack([jnp.sum(residual * residual, axis=1), jnp.sum(directi...]
  transfers between devices with their start and end apart: 14 -> 4, of which waited for: 6 -> 4; matrix products, arithmetic and copies ran while one was open for 5% -> 0% of each run, Pallas kernels for 0% -> 0%
where the time goes in v1:
time: 208 us; the launch traced here: 206 us
  waiting for transfers between devices  139 us (67%)
  Pallas kernels  26.8 us (13%)
  between operations  13.8 us (7%)
  local copies, waits for them, and re-layouts  9.91 us (5%)
  blocking collectives  8.9 us (4%)
  other arithmetic  7.22 us (3%)
    all_gather x2, waiting for transfers between devices, gather_window(): whole = lax.all_gather(block, ('row', 'col'), axis=0, tiled=False)  87.8 us
    pallas_call x2, Pallas kernels, window_product(): pl.pallas_call(functools.partial(product_kernel, tile_rows, slots, tile_s...  26.8 us
    reduce_scatter x1, waiting for transfers between devices, local(): lax.psum_scatter(window_product(known_all, ld_tiles, place, live), 'col',...  25.6 us
    reduce_scatter x1, waiting for transfers between devices, local(): lax.psum_scatter(window_product(masked_all, ld_tiles, place, live), 'col'...  25.5 us
    unnamed x22, local copies, waits for them, and re-layouts  9.91 us
    psum x1, blocking collectives, local(): lax.psum(jnp.stack([jnp.sum(residual * residual, axis=1), jnp.sum(directi...  8.9 us
  transfers between devices with their start and end apart: 4, of which 4 were waited for; matrix products, arithmetic and copies ran while one was open for 0% of the time, Pallas kernels for 0%

profile of v1, /device:TPU:12, one launch (start us, length us, event | category | flops | bytes accessed | tf_op | source)
XLA Modules:
  0.0 205.8 jit_solution(7590210405077419891)
XLA Ops:
  7.2 0.0 all-gather.5.cloned.1.call-start
  7.2 0.7 convert_element_type.9
  7.9 1.7 multiply_convert_fusion.1
  9.6 0.0 all-gather.5.cloned.1.call-update
  9.6 0.0 reduce-scatter.3.cloned.1.call-start
  9.7 0.7 subtract_clamp_fusion.live_ref
  10.3 44.7 %all-gather.5.cloned.1.call-done = bf16[1024,1280]{1,0:T(8,128)(2,1)} async-done(((bf16[64,1280]{1,0:T(8,128)(2,1)}), bf16[1024,1280]{1,0:T(8,128)(2,1)}) %all-gather.5.cloned.1.call-update) | async-done | bytes 2621456 | tf_op jit(solution)/shard_map/all_gather | solution.py:22
  55.0 0.0 copy-start
  55.0 2.9 %copy-done = bf16[5,10,256,256]{3,2,1,0:T(8,128)(2,1)S(1)} copy-done((bf16[5,10,256,256]{3,2,1,0:T(8,128)(2,1)S(1)}, bf16[5,10,256,256]{3,2,1,0:T(8,128)(2,1)}, u32[]{:S(2)}) %copy-start) | copy-done | bytes 6553624
  57.9 0.0 copy-start.2
  57.9 1.7 copy-done.2
  59.6 0.0 copy-start.4
  59.6 0.7 copy-done.4
  60.3 0.0 copy-start.6
  60.3 0.0 copy-start.7
  60.3 13.4 %window_product.2 = f32[4,64,1280]{2,1,0:T(8,128)} custom-call(s32[5,10]{1,0:T(8,128)S(1)} %copy-done.4, s32[5]{0:T(128)S(1)} %subtract_clamp_fusion.live_ref, bf16[4,4,64,1280]{3,2,1,0:T(8,128)(2,1)S(1)} %bitcast.37, bf16[5,10,256,256]{3,2,1,0:T(8,128)(2,1)S(1)} %copy-done), custom_call_target="tpu_custom_call" | custom-call | flops 1677721600 | bytes 10485760 | tf_op jit(solution)/shard_map/window_product/pallas_call | solution.py:56
  73.7 0.0 copy-start.9
  73.7 0.0 copy-start.5
  73.7 0.0 reduce-scatter.3.cloned.1.call-update
  73.7 0.0 all-gather.7.cloned.1.call-start
  73.8 25.5 %reduce-scatter.3.cloned.1.call-done = f32[1,64,1280]{2,1,0:T(8,128)} async-done(((f32[4,64,1280]{2,1,0:T(8,128)}), f32[1,64,1280]{2,1,0:T(8,128)}) %reduce-scatter.3.cloned.1.call-update) | async-done | bytes 327696 | tf_op jit(solution)/shard_map/reduce_scatter | solution.py:91
  99.3 0.0 copy-done.6
  99.3 0.0 copy-done.7
  99.3 1.3 multiply_reduce_fusion.3
  100.6 8.9 %psum.7 = f32[4,64]{1,0:T(4,128)S(1)} all-reduce(f32[4,64]{1,0:T(4,128)S(1)} %pad_maximum_fusion), channel_id=1, replica_groups=mesh['seg'=2,'row'=4,'col'=4] {'row'}, use_global_device_ids=true, to_apply=%region_5.6 | all-reduce | flops 256 | bytes 2048 | tf_op jit(solution)/shard_map/psum | solution.py:95
  109.5 0.0 copy-done.9
  109.5 1.1 multiply_add_fusion
  110.6 0.0 all-gather.7.cloned.1.call-update
  110.6 0.0 reduce-scatter.5.cloned.1.call-start
  110.7 43.1 %all-gather.7.cloned.1.call-done = bf16[1024,1280]{1,0:T(8,128)(2,1)} async-done(((bf16[64,1280]{1,0:T(8,128)(2,1)}), bf16[1024,1280]{1,0:T(8,128)(2,1)}) %all-gather.7.cloned.1.call-update) | async-done | bytes 2621456 | tf_op jit(solution)/shard_map/all_gather | solution.py:22
  153.8 0.0 copy-done.5
  153.8 0.0 copy-start.1
  153.8 2.9 %copy-done.1 = bf16[5,10,256,256]{3,2,1,0:T(8,128)(2,1)S(1)} copy-done((bf16[5,10,256,256]{3,2,1,0:T(8,128)(2,1)S(1)}, bf16[5,10,256,256]{3,2,1,0:T(8,128)(2,1)}, u32[]{:S(2)}) %copy-start.1) | copy-done | bytes 6553624
  156.7 0.0 copy-start.3
  156.7 1.7 copy-done.3
  158.4 0.0 copy-start.10
  158.4 0.0 copy-start.8
  158.4 13.4 %window_product.3 = f32[4,64,1280]{2,1,0:T(8,128)} custom-call(s32[5,10]{1,0:T(8,128)S(1)} %copy-done.5, s32[5]{0:T(128)S(1)} %subtract_clamp_fusion.live_ref, bf16[4,4,64,1280]{3,2,1,0:T(8,128)(2,1)S(1)} %bitcast.38, bf16[5,10,256,256]{3,2,1,0:T(8,128)(2,1)S(1)} %copy-done.1), custom_call_target="tpu_custom_call" | custom-call | flops 1677721600 | bytes 10485760 | tf_op jit(solution)/shard_map/window_product/pallas_call | solution.py:56
  171.8 0.0 reduce-scatter.5.cloned.1.call-update
  171.9 0.0 copy-done.10
  171.9 25.6 %reduce-scatter.5.cloned.1.call-done = f32[1,64,1280]{2,1,0:T(8,128)} async-done(((f32[4,64,1280]{2,1,0:T(8,128)}), f32[1,64,1280]{2,1,0:T(8,128)}) %reduce-scatter.5.cloned.1.call-update) | async-done | bytes 327696 | tf_op jit(solution)/shard_map/reduce_scatter | solution.py:111
  197.4 0.0 copy-done.8
  197.5 1.8 fusion
  (3 shorter events, 0.0 us)
Async XLA Ops:
  7.2 47.8 %all-gather.5.cloned.1.call-start = ((), (), s32[]{:S(2)}) async-start(), calls=%async_computation.4 | async-start | bytes 2785280 | tf_op jit(solution)/shard_map/all_gather | solution.py:22
  9.6 89.7 %reduce-scatter.3.cloned.1.call-start = ((), (), s32[]{:S(2)}) async-start(), calls=%async_computation.2 | async-start | bytes 1638400 | tf_op jit(solution)/shard_map/reduce_scatter | solution.py:91
  55.0 2.9 %copy-start = (bf16[5,10,256,256]{3,2,1,0:T(8,128)(2,1)S(1)}, bf16[5,10,256,256]{3,2,1,0:T(8,128)(2,1)}, u32[]{:S(2)}) copy-start(bf16[5,10,256,256]{3,2,1,0:T(8,128)(2,1)} %ld_ref.3) | copy-start | bytes 19660804
  57.9 1.7 copy-start.2
  59.6 0.7 copy-start.4
  60.3 39.0 %copy-start.6 = (f32[64,1280]{1,0:T(8,128)S(1)}, f32[64,1280]{1,0:T(8,128)}, u32[]{:S(2)}) copy-start(f32[64,1280]{1,0:T(8,128)} %param.13) | copy-start | bytes 983044
  60.3 39.0 %copy-start.7 = (f32[64,1280]{1,0:T(8,128)S(1)}, f32[64,1280]{1,0:T(8,128)}, u32[]{:S(2)}) copy-start(f32[64,1280]{1,0:T(8,128)} %param.12) | copy-start | bytes 983044
  73.7 35.8 %copy-start.9 = (f32[64,1280]{1,0:T(8,128)S(1)}, f32[64,1280]{1,0:T(8,128)}, u32[]{:S(2)}) copy-start(f32[64,1280]{1,0:T(8,128)} %param.11) | copy-start | bytes 983044
  73.7 80.1 %copy-start.5 = (s32[5,10]{1,0:T(8,128)S(1)}, s32[5,10]{1,0:T(8,128)}, u32[]{:S(2)}) copy-start(s32[5,10]{1,0:T(8,128)} %place_ref.3) | copy-start | bytes 604
  73.7 80.1 %all-gather.7.cloned.1.call-start = ((), (), s32[]{:S(2)}) async-start(), calls=%async_computation.5 | async-start | bytes 2785280 | tf_op jit(solution)/shard_map/all_gather | solution.py:22
  110.6 86.8 %reduce-scatter.5.cloned.1.call-start = ((), (), s32[]{:S(2)}) async-start(), calls=%async_computation.3 | async-start | bytes 1638400 | tf_op jit(solution)/shard_map/reduce_scatter | solution.py:111
  153.8 2.9 %copy-start.1 = (bf16[5,10,256,256]{3,2,1,0:T(8,128)(2,1)S(1)}, bf16[5,10,256,256]{3,2,1,0:T(8,128)(2,1)}, u32[]{:S(2)}) copy-start(bf16[5,10,256,256]{3,2,1,0:T(8,128)(2,1)} %ld_ref.3) | copy-start | bytes 19660804
  156.7 1.7 copy-start.3
  158.4 13.4 %copy-start.10 = (s32[1280]{0:T(1024)S(1)}, s32[1280]{0:T(1024)}, u32[]{:S(2)}) copy-start(s32[1280]{0:T(1024)} %param.10) | copy-start | bytes 15364
  158.4 39.0 %copy-start.8 = (f32[1,64,1280]{2,1,0:T(8,128)S(1)}, f32[1,64,1280]{2,1,0:T(8,128)}, u32[]{:S(2)}) copy-start(f32[1,64,1280]{2,1,0:T(8,128)} %reduce-scatter.3.cloned.1.call-done) | copy-start | bytes 983044
Sparse Core Ops, SparseCore 0:
  10.9 44.1 all-gather.4
  73.9 25.4 reduce-scatter.2
  110.8 43.0 all-gather.6
  172.0 25.4 reduce-scatter.4

commit v2 on v1

v2 whole, which is shorter than its diff:
```python
import functools

import jax
import jax.numpy as jnp
from jax import lax
from jax.experimental import pallas as pl
from jax.experimental.pallas import tpu as pltpu
from jax.sharding import PartitionSpec as P

W = 40


def shifted(block, axis, distance):
    size = lax.axis_size(axis)
    return lax.ppermute(block, axis, [(i, (i + distance) % size) for i in range(size)])


def swapped(block, axis, bit):
    size = lax.axis_size(axis)
    return lax.ppermute(block, axis, [(i, i ^ bit) for i in range(size)])


def row_offsets():
    return lax.axis_size("row")


def product_kernel(counts, place_ref, near_ref, far_ref, *refs):
    pieces, groups, depth, tile_size, slots = counts
    parts = refs[: pieces * groups]
    out_refs = refs[pieces * groups : pieces * groups + groups]
    held, sems = refs[pieces * groups + groups :]
    t = pl.program_id(0)
    traits = groups * depth

    @pl.when(t == 0)
    def _():
        copies = [
            pltpu.make_async_copy(
                parts[g * pieces + p], held.at[p, pl.ds(g * depth, depth)], sems.at[g * pieces + p]
            )
            for g in range(groups)
            for p in range(pieces)
        ]
        for copy in copies:
            copy.start()
        held[pieces, :, pl.ds(0, tile_size)] = jnp.zeros((traits, tile_size), held.dtype)
        for copy in copies:
            copy.wait()

    total = jnp.zeros((traits, tile_size), jnp.float32)
    for s in range(2 * slots):
        piece = place_ref[0, t, s]
        start = pl.multiple_of(place_ref[1, t, s], tile_size)
        picked = held[piece, :, pl.ds(start, tile_size)]
        tile = near_ref[0, s] if s < slots else far_ref[0, s - slots]
        total = total + lax.dot_general(
            picked, tile, (((1,), (1,)), ((), ())), preferred_element_type=jnp.float32
        )
    for g in range(groups):
        out_refs[g][...] = total[g * depth : (g + 1) * depth]


def window_product(groups, near, far, place):
    tile_rows, slots, tile_size, _ = near.shape
    pieces = len(groups[0])
    depth, width = groups[0][0].shape
    count = len(groups)
    counts = (pieces, count, depth, tile_size, slots)
    ld_spec = pl.BlockSpec((1, slots, tile_size, tile_size), lambda t: (t, 0, 0, 0))
    return pl.pallas_call(
        functools.partial(product_kernel, counts),
        grid=(tile_rows,),
        in_specs=[pl.BlockSpec(memory_space=pltpu.SMEM), ld_spec, ld_spec]
        + [pl.BlockSpec(memory_space=pl.ANY)] * (pieces * count),
        out_specs=[pl.BlockSpec((depth, tile_size), lambda t: (0, t))] * count,
        out_shape=[jax.ShapeDtypeStruct((depth, width), jnp.float32)] * count,
        scratch_shapes=[
            pltpu.VMEM((pieces + 1, count * depth, width), jnp.bfloat16),
            pltpu.SemaphoreType.DMA((pieces * count,)),
        ],
        compiler_params=pltpu.CompilerParams(vmem_limit_bytes=48 * 1024 * 1024),
        cost_estimate=pl.CostEstimate(
            flops=4 * count * depth * tile_rows * slots * tile_size**2,
            bytes_accessed=4 * near.size + (2 * pieces + 4) * count * depth * width,
            transcendentals=0,
        ),
        name="window_product",
    )(place, near, far, *[part for group in groups for part in group])


def local(ld_tiles, tile_lists, live_counts, typed_mask, solution, residual, direction):
    tile_rows, slots = tile_lists.shape
    tile_size = ld_tiles.shape[2]
    rows, cols = lax.axis_size("row"), lax.axis_size("col")
    bits = [1 << b for b in range(1, cols.bit_length() - 1)]
    reach = (W // 2 + tile_rows - 1) // tile_rows
    if 2 * reach + 1 >= rows:
        behind = list(range(rows))
    else:
        behind = list(range(reach + 1)) + list(range(rows - reach, rows))

    def along_row(block):
        return [block if d == 0 else shifted(block, "row", d) for d in behind]

    def along_col(parts):
        groups = [parts]
        for bit in bits:
            groups = groups + [[swapped(p, "col", bit) for p in g] for g in groups]
        return groups

    def summed(sums):
        for bit in reversed(bits):
            half = len(sums) // 2
            moved = [swapped(s, "col", bit) for s in sums[half:]]
            sums = [a + b for a, b in zip(sums[:half], moved)]
        return sums[0]

    typed = typed_mask.astype(jnp.float32)[None, :]
    masked = (direction * typed).astype(jnp.bfloat16)
    masked_parts = along_row(masked)
    far = swapped(ld_tiles, "col", 1)

    me = lax.axis_index("row")
    distance = lax.rem(me - tile_lists // tile_rows + rows, rows)
    piece = jnp.where(distance <= behind[len(behind) // 2], distance, distance - rows + len(behind))
    if len(behind) == rows:
        piece = distance
    slot = lax.axis_index("col") * slots + jnp.arange(slots, dtype=jnp.int32)
    live = slot[None, :] < live_counts[:, None]
    place = jnp.stack([
        jnp.where(live, piece, len(behind)),
        jnp.where(live, (tile_lists % tile_rows) * tile_size, 0),
    ])
    place = jnp.concatenate([place, swapped(place, "col", 1)], axis=2)

    masked_groups = along_col(masked_parts)
    known = (solution * typed).astype(jnp.bfloat16)
    known, *masked_parts = lax.optimization_barrier((known, *masked_parts))
    known_groups = along_col(along_row(known))

    spread = summed(window_product(masked_groups, ld_tiles, far, place))
    image = typed * direction + typed * spread + 0.1 * direction
    sums = jnp.stack([
        jnp.sum(residual * residual, axis=1),
        jnp.sum(direction * image, axis=1),
        jnp.sum(residual * image, axis=1),
        jnp.sum(image * image, axis=1),
    ])
    if rows <= 4:
        total = sums
        for d in range(1, rows):
            total = total + shifted(sums, "row", d)
    else:
        total = lax.psum(sums, "row")
    before, curve, cross, square = total
    alpha = before / curve
    after = before + alpha * (alpha * square - 2.0 * cross)
    beta = after / before
    alpha, beta = alpha[:, None], beta[:, None]
    solution_next = solution + alpha * direction
    residual_next = residual - alpha * image
    direction_next = residual_next + beta * direction
    held = summed(window_product(known_groups, ld_tiles, far, place))
    imputed = (1.0 - typed) * (held + alpha * spread)
    return (solution_next, residual_next, direction_next, imputed)


def solution(mesh):
    in_specs = (
        P(("seg", "row"), "col", None, None),
        P(("seg", "row"), "col"),
        P(("seg", "row")),
        P(("seg", "row")),
        P(("seg", "col"), "row"),
        P(("seg", "col"), "row"),
        P(("seg", "col"), "row"),
    )
    out_specs = (P(("seg", "col"), "row"),) * 4
    return jax.shard_map(local, mesh=mesh, in_specs=in_specs, out_specs=out_specs, check_vma=False)
```

time: 208 us -> 97 us (0.47)
  waiting for transfers between devices: 139 us -> 40 us
  starting transfers between devices: 0.16 us -> 31.2 us
  between operations: 13.8 us -> 0.72 us
  local copies, waits for them, and re-layouts: 9.91 us -> 0.01 us
  blocking collectives: 8.9 us -> 0 us
  Pallas kernels: 26.8 us -> 19.9 us
  other arithmetic: 7.22 us -> 4.79 us
    all_gather x2 -> x0, waiting for transfers between devices: 87.8 us -> none  [gather_window(): whole = lax.all_gather(block, ('row', 'col'), axis=0, tiled=False)]
    reduce_scatter x2 -> x0, waiting for transfers between devices: 51.1 us -> none  [the longest x1 25.6 us: local(): lax.psum_scatter(window_product(known_all, ld_tiles, place, live), 'col',...]
    ppermute x0 -> x21, waiting for transfers between devices: none -> 40 us  [the longest x12 28.2 us: swapped(): return lax.ppermute(block, axis, [(i, i ^ bit) for i in range(size)])]
    ppermute x0 -> x21, starting transfers between devices: none -> 31.2 us  [the longest x9 16 us: shifted(): lax.ppermute(block, axis, [(i, (i + distance) % size) for i in range(size)])]
    unnamed x22 -> x8, local copies, waits for them, and re-layouts: 9.91 us -> 0.01 us
    psum x1 -> x0, blocking collectives: 8.9 us -> none  [local(): lax.psum(jnp.stack([jnp.sum(residual * residual, axis=1), jnp.sum(directi...]
    pallas_call x2, Pallas kernels: 26.8 us -> 19.9 us  [window_product(): pl.pallas_call(functools.partial(product_kernel, counts), grid=(tile_rows...]
  transfers between devices with their start and end apart: 4 -> 21, of which waited for: 4 -> 15; matrix products, arithmetic and copies ran while one was open for 0% -> 3% of each run, Pallas kernels for 0% -> 0%
where the time goes in v2:
time: 97 us; the launch traced here: 96.6 us
  waiting for transfers between devices  40 us (41%)
  starting transfers between devices  31.2 us (32%)
  Pallas kernels  19.9 us (21%)
  other arithmetic  4.79 us (5%)
    ppermute x12, waiting for transfers between devices, swapped(): return lax.ppermute(block, axis, [(i, i ^ bit) for i in range(size)])  28.2 us
    pallas_call x2, Pallas kernels, window_product(): pl.pallas_call(functools.partial(product_kernel, counts), grid=(tile_rows...  19.9 us
    ppermute x9, starting transfers between devices, shifted(): lax.ppermute(block, axis, [(i, (i + distance) % size) for i in range(size)])  16 us
    ppermute x12, starting transfers between devices, swapped(): return lax.ppermute(block, axis, [(i, i ^ bit) for i in range(size)])  15.2 us
    ppermute x9, waiting for transfers between devices, shifted(): lax.ppermute(block, axis, [(i, (i + distance) % size) for i in range(size)])  11.7 us
  transfers between devices with their start and end apart: 21, of which 15 were waited for; matrix products, arithmetic and copies ran while one was open for 3% of the time, Pallas kernels for 0%

profile of v2, /device:TPU:12, one launch (start us, length us, event | category | flops | bytes accessed | tf_op | source)
XLA Modules:
  0.0 96.6 jit_solution(12982674301342849647)
XLA Ops:
  0.6 0.1 collective-permute-start.1
  0.7 0.7 convert_element_type.9
  1.4 1.0 %multiply_convert_fusion.1.refs_0_ = bf16[64,1280]{1,0:T(8,128)(2,1)S(1)} fusion(f32[64,1280]{1,0:T(8,128)} %param.13, f32[1280]{0:T(1024)S(1)} %convert_element_type.9), kind=kLoop, calls=%fused_computation.10 | loop fusion | flops 163840 | bytes 496640 | tf_op jit(solution)/shard_map/convert_element_type | solution.py:119
  2.4 1.6 %collective-permute-start.2 = (bf16[64,1280]{1,0:T(8,128)(2,1)S(1)}, bf16[64,1280]{1,0:T(8,128)(2,1)S(1)}, u32[]{:S(2)}, u32[]{:S(2)}) collective-permute-start(bf16[64,1280]{1,0:T(8,128)(2,1)S(1)} %multiply_convert_fusion.1.refs_0_), channel_id=1, source_target_pairs={{0,4},{4,8},{8,12},{12,0},{1,5},{5,9},{9,13},{13,1},{2,6},{6,10},{... | collective-permute-start | bytes 491528 | tf_op jit(solution)/shard_map/ppermute | solution.py:15
  4.0 1.2 %collective-permute-start.3 = (bf16[64,1280]{1,0:T(8,128)(2,1)S(1)}, bf16[64,1280]{1,0:T(8,128)(2,1)S(1)}, u32[]{:S(2)}, u32[]{:S(2)}) collective-permute-start(bf16[64,1280]{1,0:T(8,128)(2,1)S(1)} %multiply_convert_fusion.1.refs_0_), channel_id=1, source_target_pairs={{0,8},{4,12},{8,0},{12,4},{1,9},{5,13},{9,1},{13,5},{2,10},{6,14},... | collective-permute-start | bytes 491528 | tf_op jit(solution)/shard_map/ppermute | solution.py:15
  5.3 1.8 %collective-permute-start.4 = (bf16[64,1280]{1,0:T(8,128)(2,1)S(1)}, bf16[64,1280]{1,0:T(8,128)(2,1)S(1)}, u32[]{:S(2)}, u32[]{:S(2)}) collective-permute-start(bf16[64,1280]{1,0:T(8,128)(2,1)S(1)} %multiply_convert_fusion.1.refs_0_), channel_id=1, source_target_pairs={{0,12},{4,0},{8,4},{12,8},{1,13},{5,1},{9,5},{13,9},{2,14},{6,2},{... | collective-permute-start | bytes 491528 | tf_op jit(solution)/shard_map/ppermute | solution.py:15
  7.1 0.8 fusion
  7.8 0.0 collective-permute-start
  7.9 3.4 %collective-permute-done = s32[2,5,10]{2,1,0:T(8,128)S(1)} collective-permute-done((s32[2,5,10]{2,1,0:T(8,128)S(1)}, s32[2,5,10]{2,1,0:T(8,128)S(1)}, u32[]{:S(2)}, u32[]{:S(2)}) %collective-permute-start) | collective-permute-done | bytes 432 | tf_op jit(solution)/shard_map/ppermute | solution.py:20
  11.2 1.5 %collective-permute-start.5 = (bf16[64,1280]{1,0:T(8,128)(2,1)S(1)}, bf16[64,1280]{1,0:T(8,128)(2,1)S(1)}, u32[]{:S(2)}, u32[]{:S(2)}) collective-permute-start(bf16[64,1280]{1,0:T(8,128)(2,1)S(1)} %multiply_convert_fusion.1.refs_0_), channel_id=1, source_target_pairs={{0,2},{1,3},{2,0},{3,1},{4,6},{5,7},{6,4},{7,5},{8,10},{9,11},{10,... | collective-permute-start | bytes 491528 | tf_op jit(solution)/shard_map/ppermute | solution.py:20
  12.7 2.7 %collective-permute-done.2.refs_1_ = bf16[64,1280]{1,0:T(8,128)(2,1)S(1)} collective-permute-done((bf16[64,1280]{1,0:T(8,128)(2,1)S(1)}, bf16[64,1280]{1,0:T(8,128)(2,1)S(1)}, u32[]{:S(2)}, u32[]{:S(2)}) %collective-permute-start.2) | collective-permute-done | bytes 163872 | tf_op jit(solution)/shard_map/ppermute | solution.py:15
  15.4 1.5 %collective-permute-start.6 = (bf16[64,1280]{1,0:T(8,128)(2,1)S(1)}, bf16[64,1280]{1,0:T(8,128)(2,1)S(1)}, u32[]{:S(2)}, u32[]{:S(2)}) collective-permute-start(bf16[64,1280]{1,0:T(8,128)(2,1)S(1)} %collective-permute-done.2.refs_1_), channel_id=1, source_target_pairs={{0,2},{1,3},{2,0},{3,1},{4,6},{5,7},{6,4},{7,5},{8,10},{9,11},{10,... | collective-permute-start | bytes 491528 | tf_op jit(solution)/shard_map/ppermute | solution.py:20
  16.9 1.8 %collective-permute-done.3.refs_2_ = bf16[64,1280]{1,0:T(8,128)(2,1)S(1)} collective-permute-done((bf16[64,1280]{1,0:T(8,128)(2,1)S(1)}, bf16[64,1280]{1,0:T(8,128)(2,1)S(1)}, u32[]{:S(2)}, u32[]{:S(2)}) %collective-permute-start.3) | collective-permute-done | bytes 163872 | tf_op jit(solution)/shard_map/ppermute | solution.py:15
  18.7 1.5 %collective-permute-start.7 = (bf16[64,1280]{1,0:T(8,128)(2,1)S(1)}, bf16[64,1280]{1,0:T(8,128)(2,1)S(1)}, u32[]{:S(2)}, u32[]{:S(2)}) collective-permute-start(bf16[64,1280]{1,0:T(8,128)(2,1)S(1)} %collective-permute-done.3.refs_2_), channel_id=1, source_target_pairs={{0,2},{1,3},{2,0},{3,1},{4,6},{5,7},{6,4},{7,5},{8,10},{9,11},{10,... | collective-permute-start | bytes 491528 | tf_op jit(solution)/shard_map/ppermute | solution.py:20
  20.2 0.3 collective-permute-done.4.refs_3_
  20.4 1.5 %collective-permute-start.8 = (bf16[64,1280]{1,0:T(8,128)(2,1)S(1)}, bf16[64,1280]{1,0:T(8,128)(2,1)S(1)}, u32[]{:S(2)}, u32[]{:S(2)}) collective-permute-start(bf16[64,1280]{1,0:T(8,128)(2,1)S(1)} %collective-permute-done.4.refs_3_), channel_id=1, source_target_pairs={{0,2},{1,3},{2,0},{3,1},{4,6},{5,7},{6,4},{7,5},{8,10},{9,11},{10,... | collective-permute-start | bytes 491528 | tf_op jit(solution)/shard_map/ppermute | solution.py:20
  21.9 0.1 pad_add_fusion.1.place_ref
  22.0 0.0 collective-permute-done.5.refs_4_
  22.0 0.0 collective-permute-done.6.refs_5_
  22.0 3.8 %collective-permute-done.7.refs_6_ = bf16[64,1280]{1,0:T(8,128)(2,1)S(1)} collective-permute-done((bf16[64,1280]{1,0:T(8,128)(2,1)S(1)}, bf16[64,1280]{1,0:T(8,128)(2,1)S(1)}, u32[]{:S(2)}, u32[]{:S(2)}) %collective-permute-start.7) | collective-permute-done | bytes 163872 | tf_op jit(solution)/shard_map/ppermute | solution.py:20
  25.8 2.2 %collective-permute-done.8.refs_7_ = bf16[64,1280]{1,0:T(8,128)(2,1)S(1)} collective-permute-done((bf16[64,1280]{1,0:T(8,128)(2,1)S(1)}, bf16[64,1280]{1,0:T(8,128)(2,1)S(1)}, u32[]{:S(2)}, u32[]{:S(2)}) %collective-permute-start.8) | collective-permute-done | bytes 163872 | tf_op jit(solution)/shard_map/ppermute | solution.py:20
  28.0 0.0 collective-permute-done.1.far_ref
  28.0 10.0 %window_product.2 = (f32[64,1280]{1,0:T(8,128)S(1)}, f32[64,1280]{1,0:T(8,128)S(1)}) custom-call(s32[2,5,20]{2,1,0:T(8,128)S(1)} %pad_add_fusion.1.place_ref, bf16[5,10,256,256]{3,2,1,0:T(8,128)(2,1)} %near_ref.3, bf16[5,10,256,256]{3,2,1,0:T(8,128)(2,1)} %collective-permute-done.1.far_ref, bf16[64,1280]{1,0:T(8,128)(2,1)S(1)} %multiply_convert_fusion.1.refs_0_, ...), custom_call_target="tpu_custom_call" | custom-call | flops 1677721600 | bytes 15073280 | tf_op jit(solution)/shard_map/window_product/pallas_call | solution.py:70
  38.0 1.6 %collective-permute-start.9 = (f32[64,1280]{1,0:T(8,128)S(1)}, f32[64,1280]{1,0:T(8,128)S(1)}, u32[]{:S(2)}, u32[]{:S(2)}) collective-permute-start(f32[64,1280]{1,0:T(8,128)S(1)} %get-tuple-element.10), channel_id=1, source_target_pairs={{0,2},{1,3},{2,0},{3,1},{4,6},{5,7},{6,4},{7,5},{8,10},{9,11},{10,... | collective-permute-start | bytes 983048 | tf_op jit(solution)/shard_map/ppermute | solution.py:20
  39.5 7.0 %collective-permute-done.9 = f32[64,1280]{1,0:T(8,128)S(1)} collective-permute-done((f32[64,1280]{1,0:T(8,128)S(1)}, f32[64,1280]{1,0:T(8,128)S(1)}, u32[]{:S(2)}, u32[]{:S(2)}) %collective-permute-start.9) | collective-permute-done | bytes 327712 | tf_op jit(solution)/shard_map/ppermute | solution.py:20
  46.5 0.3 multiply_reduce_fusion.3
  46.8 1.2 %collective-permute-start.12 = (f32[4,64]{1,0:T(4,128)S(1)}, f32[4,64]{1,0:T(4,128)S(1)}, u32[]{:S(2)}, u32[]{:S(2)}) collective-permute-start(f32[4,64]{1,0:T(4,128)S(1)} %pad_maximum_fusion), channel_id=1, source_target_pairs={{0,12},{4,0},{8,4},{12,8},{1,13},{5,1},{9,5},{13,9},{2,14},{6,2},{... | collective-permute-start | bytes 3080 | tf_op jit(solution)/shard_map/ppermute | solution.py:15
  48.0 2.3 %collective-permute-start.11 = (f32[4,64]{1,0:T(4,128)S(1)}, f32[4,64]{1,0:T(4,128)S(1)}, u32[]{:S(2)}, u32[]{:S(2)}) collective-permute-start(f32[4,64]{1,0:T(4,128)S(1)} %pad_maximum_fusion), channel_id=1, source_target_pairs={{0,8},{4,12},{8,0},{12,4},{1,9},{5,13},{9,1},{13,5},{2,10},{6,14},... | collective-permute-start | bytes 3080 | tf_op jit(solution)/shard_map/ppermute | solution.py:15
  50.3 2.8 %collective-permute-start.10 = (f32[4,64]{1,0:T(4,128)S(1)}, f32[4,64]{1,0:T(4,128)S(1)}, u32[]{:S(2)}, u32[]{:S(2)}) collective-permute-start(f32[4,64]{1,0:T(4,128)S(1)} %pad_maximum_fusion), channel_id=1, source_target_pairs={{0,4},{4,8},{8,12},{12,0},{1,5},{5,9},{9,13},{13,1},{2,6},{6,10},{... | collective-permute-start | bytes 3080 | tf_op jit(solution)/shard_map/ppermute | solution.py:15
  53.1 1.3 %collective-permute-done.10 = f32[4,64]{1,0:T(4,128)S(1)} collective-permute-done((f32[4,64]{1,0:T(4,128)S(1)}, f32[4,64]{1,0:T(4,128)S(1)}, u32[]{:S(2)}, u32[]{:S(2)}) %collective-permute-start.10) | collective-permute-done | bytes 1056 | tf_op jit(solution)/shard_map/ppermute | solution.py:15
  54.5 1.1 %multiply_add_fusion = (f32[64,1280]{1,0:T(8,128)}, f32[64,1280]{1,0:T(8,128)}, f32[64,1280]{1,0:T(8,128)}, bf16[64,1280]{1,0:T(8,128)(2,1)S(1)}) fusion(f32[64,1280]{1,0:T(8,128)S(1)} %copy-done, f32[64]{0:T(128)S(1)} %get-tuple-element.20, f32[64,1280]{1,0:T(8,128)S(1)} %copy-done.1, f32[64,1280]{1,0:T(8,128)S(1)} %get-tuple-element.22, ...), kind=kLoop, calls=%fused_computation.2 | loop fusion | flops 655360 | bytes 2463232 | tf_op jit(solution)/shard_map/add | solution.py:162
  55.6 2.3 %collective-permute-start.13 = (bf16[64,1280]{1,0:T(8,128)(2,1)S(1)}, bf16[64,1280]{1,0:T(8,128)(2,1)S(1)}, u32[]{:S(2)}, u32[]{:S(2)}) collective-permute-start(bf16[64,1280]{1,0:T(8,128)(2,1)S(1)} %get-tuple-element.11.refs_0_), channel_id=1, source_target_pairs={{0,4},{4,8},{8,12},{12,0},{1,5},{5,9},{9,13},{13,1},{2,6},{6,10},{... | collective-permute-start | bytes 491528 | tf_op jit(solution)/shard_map/ppermute | solution.py:15
  57.9 2.7 %collective-permute-start.14 = (bf16[64,1280]{1,0:T(8,128)(2,1)S(1)}, bf16[64,1280]{1,0:T(8,128)(2,1)S(1)}, u32[]{:S(2)}, u32[]{:S(2)}) collective-permute-start(bf16[64,1280]{1,0:T(8,128)(2,1)S(1)} %get-tuple-element.11.refs_0_), channel_id=1, source_target_pairs={{0,8},{4,12},{8,0},{12,4},{1,9},{5,13},{9,1},{13,5},{2,10},{6,14},... | collective-permute-start | bytes 491528 | tf_op jit(solution)/shard_map/ppermute | solution.py:15
  60.6 0.0 collective-permute-start.15
  60.6 1.5 %collective-permute-start.16 = (bf16[64,1280]{1,0:T(8,128)(2,1)S(1)}, bf16[64,1280]{1,0:T(8,128)(2,1)S(1)}, u32[]{:S(2)}, u32[]{:S(2)}) collective-permute-start(bf16[64,1280]{1,0:T(8,128)(2,1)S(1)} %get-tuple-element.11.refs_0_), channel_id=1, source_target_pairs={{0,2},{1,3},{2,0},{3,1},{4,6},{5,7},{6,4},{7,5},{8,10},{9,11},{10,... | collective-permute-start | bytes 491528 | tf_op jit(solution)/shard_map/ppermute | solution.py:20
  62.1 4.7 %collective-permute-done.13.refs_1_ = bf16[64,1280]{1,0:T(8,128)(2,1)S(1)} collective-permute-done((bf16[64,1280]{1,0:T(8,128)(2,1)S(1)}, bf16[64,1280]{1,0:T(8,128)(2,1)S(1)}, u32[]{:S(2)}, u32[]{:S(2)}) %collective-permute-start.13) | collective-permute-done | bytes 163872 | tf_op jit(solution)/shard_map/ppermute | solution.py:15
  66.8 1.5 %collective-permute-start.17 = (bf16[64,1280]{1,0:T(8,128)(2,1)S(1)}, bf16[64,1280]{1,0:T(8,128)(2,1)S(1)}, u32[]{:S(2)}, u32[]{:S(2)}) collective-permute-start(bf16[64,1280]{1,0:T(8,128)(2,1)S(1)} %collective-permute-done.13.refs_1_), channel_id=1, source_target_pairs={{0,2},{1,3},{2,0},{3,1},{4,6},{5,7},{6,4},{7,5},{8,10},{9,11},{10,... | collective-permute-start | bytes 491528 | tf_op jit(solution)/shard_map/ppermute | solution.py:20
  68.3 0.2 collective-permute-done.14.refs_2_
  68.6 1.5 %collective-permute-start.18 = (bf16[64,1280]{1,0:T(8,128)(2,1)S(1)}, bf16[64,1280]{1,0:T(8,128)(2,1)S(1)}, u32[]{:S(2)}, u32[]{:S(2)}) collective-permute-start(bf16[64,1280]{1,0:T(8,128)(2,1)S(1)} %collective-permute-done.14.refs_2_), channel_id=1, source_target_pairs={{0,2},{1,3},{2,0},{3,1},{4,6},{5,7},{6,4},{7,5},{8,10},{9,11},{10,... | collective-permute-start | bytes 491528 | tf_op jit(solution)/shard_map/ppermute | solution.py:20
  70.1 0.7 collective-permute-done.15.refs_3_
  70.8 1.5 %collective-permute-start.19 = (bf16[64,1280]{1,0:T(8,128)(2,1)S(1)}, bf16[64,1280]{1,0:T(8,128)(2,1)S(1)}, u32[]{:S(2)}, u32[]{:S(2)}) collective-permute-start(bf16[64,1280]{1,0:T(8,128)(2,1)S(1)} %collective-permute-done.15.refs_3_), channel_id=1, source_target_pairs={{0,2},{1,3},{2,0},{3,1},{4,6},{5,7},{6,4},{7,5},{8,10},{9,11},{10,... | collective-permute-start | bytes 491528 | tf_op jit(solution)/shard_map/ppermute | solution.py:20
  72.3 1.0 %collective-permute-done.17.refs_5_ = bf16[64,1280]{1,0:T(8,128)(2,1)S(1)} collective-permute-done((bf16[64,1280]{1,0:T(8,128)(2,1)S(1)}, bf16[64,1280]{1,0:T(8,128)(2,1)S(1)}, u32[]{:S(2)}, u32[]{:S(2)}) %collective-permute-start.17) | collective-permute-done | bytes 163872 | tf_op jit(solution)/shard_map/ppermute | solution.py:20
  73.3 3.1 %collective-permute-done.18.refs_6_ = bf16[64,1280]{1,0:T(8,128)(2,1)S(1)} collective-permute-done((bf16[64,1280]{1,0:T(8,128)(2,1)S(1)}, bf16[64,1280]{1,0:T(8,128)(2,1)S(1)}, u32[]{:S(2)}, u32[]{:S(2)}) %collective-permute-start.18) | collective-permute-done | bytes 163872 | tf_op jit(solution)/shard_map/ppermute | solution.py:20
  76.4 1.8 %collective-permute-done.19.refs_7_ = bf16[64,1280]{1,0:T(8,128)(2,1)S(1)} collective-permute-done((bf16[64,1280]{1,0:T(8,128)(2,1)S(1)}, bf16[64,1280]{1,0:T(8,128)(2,1)S(1)}, u32[]{:S(2)}, u32[]{:S(2)}) %collective-permute-start.19) | collective-permute-done | bytes 163872 | tf_op jit(solution)/shard_map/ppermute | solution.py:20
  78.2 10.0 %window_product.3 = (f32[64,1280]{1,0:T(8,128)S(1)}, f32[64,1280]{1,0:T(8,128)S(1)}) custom-call(s32[2,5,20]{2,1,0:T(8,128)S(1)} %pad_add_fusion.1.place_ref, bf16[5,10,256,256]{3,2,1,0:T(8,128)(2,1)} %near_ref.3, bf16[5,10,256,256]{3,2,1,0:T(8,128)(2,1)} %collective-permute-done.1.far_ref, bf16[64,1280]{1,0:T(8,128)(2,1)S(1)} %get-tuple-element.11.refs_0_, ...), custom_call_target="tpu_custom_call" | custom-call | flops 1677721600 | bytes 15073280 | tf_op jit(solution)/shard_map/window_product/pallas_call | solution.py:70
  88.1 1.6 %collective-permute-start.20 = (f32[64,1280]{1,0:T(8,128)S(1)}, f32[64,1280]{1,0:T(8,128)S(1)}, u32[]{:S(2)}, u32[]{:S(2)}) collective-permute-start(f32[64,1280]{1,0:T(8,128)S(1)} %get-tuple-element.13), channel_id=1, source_target_pairs={{0,2},{1,3},{2,0},{3,1},{4,6},{5,7},{6,4},{7,5},{8,10},{9,11},{10,... | collective-permute-start | bytes 983048 | tf_op jit(solution)/shard_map/ppermute | solution.py:20
  89.7 6.1 %collective-permute-done.20 = f32[64,1280]{1,0:T(8,128)S(1)} collective-permute-done((f32[64,1280]{1,0:T(8,128)S(1)}, f32[64,1280]{1,0:T(8,128)S(1)}, u32[]{:S(2)}, u32[]{:S(2)}) %collective-permute-start.20) | collective-permute-done | bytes 327712 | tf_op jit(solution)/shard_map/ppermute | solution.py:20
  95.8 0.8 add_multiply_fusion
  (17 shorter events, 0.1 us)
Async XLA Ops:
  0.6 27.4 %collective-permute-start.1 = (bf16[5,10,256,256]{3,2,1,0:T(8,128)(2,1)}, bf16[5,10,256,256]{3,2,1,0:T(8,128)(2,1)}, u32[]{:S(2)}, u32[]{:S(2)}) collective-permute-start(bf16[5,10,256,256]{3,2,1,0:T(8,128)(2,1)} %near_ref.3), channel_id=1, source_target_pairs={{0,1},{1,0},{2,3},{3,2},{4,5},{5,4},{6,7},{7,6},{8,9},{9,8},{10,11... | collective-permute-start | bytes 19660808 | tf_op jit(solution)/shard_map/ppermute | solution.py:20
  2.4 13.0 %collective-permute-start.2 = (bf16[64,1280]{1,0:T(8,128)(2,1)S(1)}, bf16[64,1280]{1,0:T(8,128)(2,1)S(1)}, u32[]{:S(2)}, u32[]{:S(2)}) collective-permute-start(bf16[64,1280]{1,0:T(8,128)(2,1)S(1)} %multiply_convert_fusion.1.refs_0_), channel_id=1, source_target_pairs={{0,4},{4,8},{8,12},{12,0},{1,5},{5,9},{9,13},{13,1},{2,6},{6,10},{... | collective-permute-start | bytes 491528 | tf_op jit(solution)/shard_map/ppermute | solution.py:15
  4.0 14.6 %collective-permute-start.3 = (bf16[64,1280]{1,0:T(8,128)(2,1)S(1)}, bf16[64,1280]{1,0:T(8,128)(2,1)S(1)}, u32[]{:S(2)}, u32[]{:S(2)}) collective-permute-start(bf16[64,1280]{1,0:T(8,128)(2,1)S(1)} %multiply_convert_fusion.1.refs_0_), channel_id=1, source_target_pairs={{0,8},{4,12},{8,0},{12,4},{1,9},{5,13},{9,1},{13,5},{2,10},{6,14},... | collective-permute-start | bytes 491528 | tf_op jit(solution)/shard_map/ppermute | solution.py:15
  5.3 15.2 %collective-permute-start.4 = (bf16[64,1280]{1,0:T(8,128)(2,1)S(1)}, bf16[64,1280]{1,0:T(8,128)(2,1)S(1)}, u32[]{:S(2)}, u32[]{:S(2)}) collective-permute-start(bf16[64,1280]{1,0:T(8,128)(2,1)S(1)} %multiply_convert_fusion.1.refs_0_), channel_id=1, source_target_pairs={{0,12},{4,0},{8,4},{12,8},{1,13},{5,1},{9,5},{13,9},{2,14},{6,2},{... | collective-permute-start | bytes 491528 | tf_op jit(solution)/shard_map/ppermute | solution.py:15
  7.8 3.4 %collective-permute-start = (s32[2,5,10]{2,1,0:T(8,128)S(1)}, s32[2,5,10]{2,1,0:T(8,128)S(1)}, u32[]{:S(2)}, u32[]{:S(2)}) collective-permute-start(s32[2,5,10]{2,1,0:T(8,128)S(1)} %pad_add_fusion), channel_id=1, source_target_pairs={{0,1},{1,0},{2,3},{3,2},{4,5},{5,4},{6,7},{7,6},{8,9},{9,8},{10,11... | collective-permute-start | bytes 1208 | tf_op jit(solution)/shard_map/ppermute | solution.py:20
  11.2 10.8 %collective-permute-start.5 = (bf16[64,1280]{1,0:T(8,128)(2,1)S(1)}, bf16[64,1280]{1,0:T(8,128)(2,1)S(1)}, u32[]{:S(2)}, u32[]{:S(2)}) collective-permute-start(bf16[64,1280]{1,0:T(8,128)(2,1)S(1)} %multiply_convert_fusion.1.refs_0_), channel_id=1, source_target_pairs={{0,2},{1,3},{2,0},{3,1},{4,6},{5,7},{6,4},{7,5},{8,10},{9,11},{10,... | collective-permute-start | bytes 491528 | tf_op jit(solution)/shard_map/ppermute | solution.py:20
  15.4 6.6 %collective-permute-start.6 = (bf16[64,1280]{1,0:T(8,128)(2,1)S(1)}, bf16[64,1280]{1,0:T(8,128)(2,1)S(1)}, u32[]{:S(2)}, u32[]{:S(2)}) collective-permute-start(bf16[64,1280]{1,0:T(8,128)(2,1)S(1)} %collective-permute-done.2.refs_1_), channel_id=1, source_target_pairs={{0,2},{1,3},{2,0},{3,1},{4,6},{5,7},{6,4},{7,5},{8,10},{9,11},{10,... | collective-permute-start | bytes 491528 | tf_op jit(solution)/shard_map/ppermute | solution.py:20
  18.7 7.1 %collective-permute-start.7 = (bf16[64,1280]{1,0:T(8,128)(2,1)S(1)}, bf16[64,1280]{1,0:T(8,128)(2,1)S(1)}, u32[]{:S(2)}, u32[]{:S(2)}) collective-permute-start(bf16[64,1280]{1,0:T(8,128)(2,1)S(1)} %collective-permute-done.3.refs_2_), channel_id=1, source_target_pairs={{0,2},{1,3},{2,0},{3,1},{4,6},{5,7},{6,4},{7,5},{8,10},{9,11},{10,... | collective-permute-start | bytes 491528 | tf_op jit(solution)/shard_map/ppermute | solution.py:20
  20.4 7.6 %collective-permute-start.8 = (bf16[64,1280]{1,0:T(8,128)(2,1)S(1)}, bf16[64,1280]{1,0:T(8,128)(2,1)S(1)}, u32[]{:S(2)}, u32[]{:S(2)}) collective-permute-start(bf16[64,1280]{1,0:T(8,128)(2,1)S(1)} %collective-permute-done.4.refs_3_), channel_id=1, source_target_pairs={{0,2},{1,3},{2,0},{3,1},{4,6},{5,7},{6,4},{7,5},{8,10},{9,11},{10,... | collective-permute-start | bytes 491528 | tf_op jit(solution)/shard_map/ppermute | solution.py:20
  22.0 24.5 %copy-start = (f32[64,1280]{1,0:T(8,128)S(1)}, f32[64,1280]{1,0:T(8,128)}, u32[]{:S(2)}) copy-start(f32[64,1280]{1,0:T(8,128)} %param.13) | copy-start | bytes 983044
  22.0 24.5 %copy-start.1 = (f32[64,1280]{1,0:T(8,128)S(1)}, f32[64,1280]{1,0:T(8,128)}, u32[]{:S(2)}) copy-start(f32[64,1280]{1,0:T(8,128)} %param.12) | copy-start | bytes 983044
  22.0 32.5 %copy-start.2 = (f32[64,1280]{1,0:T(8,128)S(1)}, f32[64,1280]{1,0:T(8,128)}, u32[]{:S(2)}) copy-start(f32[64,1280]{1,0:T(8,128)} %param.11) | copy-start | bytes 983044
  38.0 8.5 %collective-permute-start.9 = (f32[64,1280]{1,0:T(8,128)S(1)}, f32[64,1280]{1,0:T(8,128)S(1)}, u32[]{:S(2)}, u32[]{:S(2)}) collective-permute-start(f32[64,1280]{1,0:T(8,128)S(1)} %get-tuple-element.10), channel_id=1, source_target_pairs={{0,2},{1,3},{2,0},{3,1},{4,6},{5,7},{6,4},{7,5},{8,10},{9,11},{10,... | collective-permute-start | bytes 983048 | tf_op jit(solution)/shard_map/ppermute | solution.py:20
  46.8 6.3 %collective-permute-start.12 = (f32[4,64]{1,0:T(4,128)S(1)}, f32[4,64]{1,0:T(4,128)S(1)}, u32[]{:S(2)}, u32[]{:S(2)}) collective-permute-start(f32[4,64]{1,0:T(4,128)S(1)} %pad_maximum_fusion), channel_id=1, source_target_pairs={{0,12},{4,0},{8,4},{12,8},{1,13},{5,1},{9,5},{13,9},{2,14},{6,2},{... | collective-permute-start | bytes 3080 | tf_op jit(solution)/shard_map/ppermute | solution.py:15
  48.0 5.1 %collective-permute-start.11 = (f32[4,64]{1,0:T(4,128)S(1)}, f32[4,64]{1,0:T(4,128)S(1)}, u32[]{:S(2)}, u32[]{:S(2)}) collective-permute-start(f32[4,64]{1,0:T(4,128)S(1)} %pad_maximum_fusion), channel_id=1, source_target_pairs={{0,8},{4,12},{8,0},{12,4},{1,9},{5,13},{9,1},{13,5},{2,10},{6,14},... | collective-permute-start | bytes 3080 | tf_op jit(solution)/shard_map/ppermute | solution.py:15
  50.3 4.2 %collective-permute-start.10 = (f32[4,64]{1,0:T(4,128)S(1)}, f32[4,64]{1,0:T(4,128)S(1)}, u32[]{:S(2)}, u32[]{:S(2)}) collective-permute-start(f32[4,64]{1,0:T(4,128)S(1)} %pad_maximum_fusion), channel_id=1, source_target_pairs={{0,4},{4,8},{8,12},{12,0},{1,5},{5,9},{9,13},{13,1},{2,6},{6,10},{... | collective-permute-start | bytes 3080 | tf_op jit(solution)/shard_map/ppermute | solution.py:15
  55.6 34.1 %copy-start.3 = (s32[1280]{0:T(1024)S(1)}, s32[1280]{0:T(1024)}, u32[]{:S(2)}) copy-start(s32[1280]{0:T(1024)} %param.10) | copy-start | bytes 15364
  55.6 11.2 %collective-permute-start.13 = (bf16[64,1280]{1,0:T(8,128)(2,1)S(1)}, bf16[64,1280]{1,0:T(8,128)(2,1)S(1)}, u32[]{:S(2)}, u32[]{:S(2)}) collective-permute-start(bf16[64,1280]{1,0:T(8,128)(2,1)S(1)} %get-tuple-element.11.refs_0_), channel_id=1, source_target_pairs={{0,4},{4,8},{8,12},{12,0},{1,5},{5,9},{9,13},{13,1},{2,6},{6,10},{... | collective-permute-start | bytes 491528 | tf_op jit(solution)/shard_map/ppermute | solution.py:15
  57.9 10.7 %collective-permute-start.14 = (bf16[64,1280]{1,0:T(8,128)(2,1)S(1)}, bf16[64,1280]{1,0:T(8,128)(2,1)S(1)}, u32[]{:S(2)}, u32[]{:S(2)}) collective-permute-start(bf16[64,1280]{1,0:T(8,128)(2,1)S(1)} %get-tuple-element.11.refs_0_), channel_id=1, source_target_pairs={{0,8},{4,12},{8,0},{12,4},{1,9},{5,13},{9,1},{13,5},{2,10},{6,14},... | collective-permute-start | bytes 491528 | tf_op jit(solution)/shard_map/ppermute | solution.py:15
  60.6 10.2 %collective-permute-start.15 = (bf16[64,1280]{1,0:T(8,128)(2,1)S(1)}, bf16[64,1280]{1,0:T(8,128)(2,1)S(1)}, u32[]{:S(2)}, u32[]{:S(2)}) collective-permute-start(bf16[64,1280]{1,0:T(8,128)(2,1)S(1)} %get-tuple-element.11.refs_0_), channel_id=1, source_target_pairs={{0,12},{4,0},{8,4},{12,8},{1,13},{5,1},{9,5},{13,9},{2,14},{6,2},{... | collective-permute-start | bytes 491528 | tf_op jit(solution)/shard_map/ppermute | solution.py:15
  60.6 11.7 %collective-permute-start.16 = (bf16[64,1280]{1,0:T(8,128)(2,1)S(1)}, bf16[64,1280]{1,0:T(8,128)(2,1)S(1)}, u32[]{:S(2)}, u32[]{:S(2)}) collective-permute-start(bf16[64,1280]{1,0:T(8,128)(2,1)S(1)} %get-tuple-element.11.refs_0_), channel_id=1, source_target_pairs={{0,2},{1,3},{2,0},{3,1},{4,6},{5,7},{6,4},{7,5},{8,10},{9,11},{10,... | collective-permute-start | bytes 491528 | tf_op jit(solution)/shard_map/ppermute | solution.py:20
  66.8 6.5 %collective-permute-start.17 = (bf16[64,1280]{1,0:T(8,128)(2,1)S(1)}, bf16[64,1280]{1,0:T(8,128)(2,1)S(1)}, u32[]{:S(2)}, u32[]{:S(2)}) collective-permute-start(bf16[64,1280]{1,0:T(8,128)(2,1)S(1)} %collective-permute-done.13.refs_1_), channel_id=1, source_target_pairs={{0,2},{1,3},{2,0},{3,1},{4,6},{5,7},{6,4},{7,5},{8,10},{9,11},{10,... | collective-permute-start | bytes 491528 | tf_op jit(solution)/shard_map/ppermute | solution.py:20
  68.6 7.8 %collective-permute-start.18 = (bf16[64,1280]{1,0:T(8,128)(2,1)S(1)}, bf16[64,1280]{1,0:T(8,128)(2,1)S(1)}, u32[]{:S(2)}, u32[]{:S(2)}) collective-permute-start(bf16[64,1280]{1,0:T(8,128)(2,1)S(1)} %collective-permute-done.14.refs_2_), channel_id=1, source_target_pairs={{0,2},{1,3},{2,0},{3,1},{4,6},{5,7},{6,4},{7,5},{8,10},{9,11},{10,... | collective-permute-start | bytes 491528 | tf_op jit(solution)/shard_map/ppermute | solution.py:20
  70.8 7.4 %collective-permute-start.19 = (bf16[64,1280]{1,0:T(8,128)(2,1)S(1)}, bf16[64,1280]{1,0:T(8,128)(2,1)S(1)}, u32[]{:S(2)}, u32[]{:S(2)}) collective-permute-start(bf16[64,1280]{1,0:T(8,128)(2,1)S(1)} %collective-permute-done.15.refs_3_), channel_id=1, source_target_pairs={{0,2},{1,3},{2,0},{3,1},{4,6},{5,7},{6,4},{7,5},{8,10},{9,11},{10,... | collective-permute-start | bytes 491528 | tf_op jit(solution)/shard_map/ppermute | solution.py:20
  88.1 7.6 %collective-permute-start.20 = (f32[64,1280]{1,0:T(8,128)S(1)}, f32[64,1280]{1,0:T(8,128)S(1)}, u32[]{:S(2)}, u32[]{:S(2)}) collective-permute-start(f32[64,1280]{1,0:T(8,128)S(1)} %get-tuple-element.13), channel_id=1, source_target_pairs={{0,2},{1,3},{2,0},{3,1},{4,6},{5,7},{6,4},{7,5},{8,10},{9,11},{10,... | collective-permute-start | bytes 983048 | tf_op jit(solution)/shard_map/ppermute | solution.py:20

commit v3 on v2

--- a/solution.py
+++ b/solution.py
@@ -20,15 +20,11 @@
     return lax.ppermute(block, axis, [(i, i ^ bit) for i in range(size)])
 
 
-def row_offsets():
-    return lax.axis_size("row")
-
-
 def product_kernel(counts, place_ref, near_ref, far_ref, *refs):
-    pieces, groups, depth, tile_size, slots = counts
+    pieces, groups, depth, tile_size, slots, tile_rows, flip = counts
     parts = refs[: pieces * groups]
     out_refs = refs[pieces * groups : pieces * groups + groups]
-    held, sems = refs[pieces * groups + groups :]
+    held, turned, sems = refs[pieces * groups + groups :]
     t = pl.program_id(0)
     traits = groups * depth
 
@@ -46,26 +42,39 @@
         held[pieces, :, pl.ds(0, tile_size)] = jnp.zeros((traits, tile_size), held.dtype)
         for copy in copies:
             copy.wait()
+        if flip:
+            for p in range(pieces):
+                for r in range(tile_rows):
+                    turned[p * tile_rows + r] = held[p, :, r * tile_size : (r + 1) * tile_size].T
+            turned[pieces * tile_rows] = jnp.zeros((tile_size, traits), held.dtype)
 
-    total = jnp.zeros((traits, tile_size), jnp.float32)
+    if flip:
+        total = jnp.zeros((tile_size, traits), jnp.float32)
+    else:
+        total = jnp.zeros((traits, tile_size), jnp.float32)
     for s in range(2 * slots):
-        piece = place_ref[0, t, s]
-        start = pl.multiple_of(place_ref[1, t, s], tile_size)
-        picked = held[piece, :, pl.ds(start, tile_size)]
         tile = near_ref[0, s] if s < slots else far_ref[0, s - slots]
-        total = total + lax.dot_general(
-            picked, tile, (((1,), (1,)), ((), ())), preferred_element_type=jnp.float32
-        )
+        if flip:
+            picked = turned[place_ref[2, t, s]]
+            total = total + jnp.dot(tile, picked, preferred_element_type=jnp.float32)
+        else:
+            start = pl.multiple_of(place_ref[1, t, s], tile_size)
+            picked = held[place_ref[0, t, s], :, pl.ds(start, tile_size)]
+            total = total + lax.dot_general(
+                picked, tile, (((1,), (1,)), ((), ())), preferred_element_type=jnp.float32
+            )
+    if flip:
+        total = total.T
     for g in range(groups):
         out_refs[g][...] = total[g * depth : (g + 1) * depth]
 
 
-def window_product(groups, near, far, place):
+def window_product(groups, near, far, place, flip):
     tile_rows, slots, tile_size, _ = near.shape
     pieces = len(groups[0])
     depth, width = groups[0][0].shape
     count = len(groups)
-    counts = (pieces, count, depth, tile_size, slots)
+    counts = (pieces, count, depth, tile_size, slots, tile_rows, flip)
     ld_spec = pl.BlockSpec((1, slots, tile_size, tile_size), lambda t: (t, 0, 0, 0))
     return pl.pallas_call(
         functools.partial(product_kernel, counts),
@@ -76,9 +85,10 @@
         out_shape=[jax.ShapeDtypeStruct((depth, width), jnp.float32)] * count,
         scratch_shapes=[
             pltpu.VMEM((pieces + 1, count * depth, width), jnp.bfloat16),
+            pltpu.VMEM((pieces * tile_rows + 1, tile_size, count * depth), jnp.bfloat16),
             pltpu.SemaphoreType.DMA((pieces * count,)),
         ],
-        compiler_params=pltpu.CompilerParams(vmem_limit_bytes=48 * 1024 * 1024),
+        compiler_params=pltpu.CompilerParams(vmem_limit_bytes=24 * 1024 * 1024),
         cost_estimate=pl.CostEstimate(
             flops=4 * count * depth * tile_rows * slots * tile_size**2,
             bytes_accessed=4 * near.size + (2 * pieces + 4) * count * depth * width,
@@ -117,8 +127,11 @@
 
     typed = typed_mask.astype(jnp.float32)[None, :]
     masked = (direction * typed).astype(jnp.bfloat16)
+    known = (solution * typed).astype(jnp.bfloat16)
+    masked, known = lax.optimization_barrier((masked, known))
     masked_parts = along_row(masked)
     far = swapped(ld_tiles, "col", 1)
+    masked_groups = along_col(masked_parts)
 
     me = lax.axis_index("row")
     distance = lax.rem(me - tile_lists // tile_rows + rows, rows)
@@ -127,18 +140,19 @@
         piece = distance
     slot = lax.axis_index("col") * slots + jnp.arange(slots, dtype=jnp.int32)
     live = slot[None, :] < live_counts[:, None]
+    inner = tile_lists % tile_rows
     place = jnp.stack([
         jnp.where(live, piece, len(behind)),
-        jnp.where(live, (tile_lists % tile_rows) * tile_size, 0),
+        jnp.where(live, inner * tile_size, 0),
+        jnp.where(live, piece * tile_rows + inner, len(behind) * tile_rows),
     ])
+    place, _ = lax.optimization_barrier((place, masked_parts[1]))
     place = jnp.concatenate([place, swapped(place, "col", 1)], axis=2)
 
-    masked_groups = along_col(masked_parts)
-    known = (solution * typed).astype(jnp.bfloat16)
-    known, *masked_parts = lax.optimization_barrier((known, *masked_parts))
+    known, *_ = lax.optimization_barrier((known, *masked_parts))
     known_groups = along_col(along_row(known))
 
-    spread = summed(window_product(masked_groups, ld_tiles, far, place))
+    spread = summed(window_product(masked_groups, ld_tiles, far, place, False))
     image = typed * direction + typed * spread + 0.1 * direction
     sums = jnp.stack([
         jnp.sum(residual * residual, axis=1),
@@ -160,7 +174,7 @@
     solution_next = solution + alpha * direction
     residual_next = residual - alpha * image
     direction_next = residual_next + beta * direction
-    held = summed(window_product(known_groups, ld_tiles, far, place))
+    held = summed(window_product(known_groups, ld_tiles, far, place, True))
     imputed = (1.0 - typed) * (held + alpha * spread)
     return (solution_next, residual_next, direction_next, imputed)
 

time: 97 us -> 91.3 us (0.941)
  starting transfers between devices: 31.2 us -> 25.7 us
  local copies, waits for them, and re-layouts: 0.01 us -> 2.88 us
  Pallas kernels: 19.9 us -> 18.1 us
    ppermute x12, waiting for transfers between devices: 28.2 us -> 18.9 us  [swapped(): return lax.ppermute(block, axis, [(i, i ^ bit) for i in range(size)])]
    ppermute x9, waiting for transfers between devices: 11.7 us -> 20.4 us  [shifted(): lax.ppermute(block, axis, [(i, (i + distance) % size) for i in range(size)])]
    ppermute x12, starting transfers between devices: 15.2 us -> 10.3 us  [swapped(): return lax.ppermute(block, axis, [(i, i ^ bit) for i in range(size)])]
    unnamed x8 -> x10, local copies, waits for them, and re-layouts: 0.01 us -> 2.88 us
    pallas_call x2, Pallas kernels: 19.9 us -> 18.1 us  [window_product(): pl.pallas_call(functools.partial(product_kernel, counts), grid=(tile_rows...]
  transfers between devices with their start and end apart: 21 -> 21, of which waited for: 15 -> 10; matrix products, arithmetic and copies ran while one was open for 3% -> 3% of each run, Pallas kernels for 0% -> 10%
where the time goes in v3:
time: 91.3 us; the launch traced here: 90.9 us
  waiting for transfers between devices  39.3 us (43%)
  starting transfers between devices  25.7 us (28%)
  Pallas kernels  18.1 us (20%)
  other arithmetic  4.17 us (5%)
  local copies, waits for them, and re-layouts  2.88 us (3%)
    ppermute x9, waiting for transfers between devices, shifted(): lax.ppermute(block, axis, [(i, (i + distance) % size) for i in range(size)])  20.4 us
    ppermute x12, waiting for transfers between devices, swapped(): return lax.ppermute(block, axis, [(i, i ^ bit) for i in range(size)])  18.9 us
    pallas_call x2, Pallas kernels, window_product(): pl.pallas_call(functools.partial(product_kernel, counts), grid=(tile_rows...  18.1 us
    ppermute x9, starting transfers between devices, shifted(): lax.ppermute(block, axis, [(i, (i + distance) % size) for i in range(size)])  15.4 us
    ppermute x12, starting transfers between devices, swapped(): return lax.ppermute(block, axis, [(i, i ^ bit) for i in range(size)])  10.3 us
    unnamed x10, local copies, waits for them, and re-layouts  2.88 us
  transfers between devices with their start and end apart: 21, of which 10 were waited for; matrix products, arithmetic and copies ran while one was open for 3% of the time, Pallas kernels for 10%

profile of v3, /device:TPU:12, one launch (start us, length us, event | category | flops | bytes accessed | tf_op | source)
XLA Modules:
  0.0 90.9 jit_solution(17547920231535447051)
XLA Ops:
  0.6 0.1 collective-permute-start.2
  0.7 0.7 convert_element_type.9
  1.4 1.1 %multiply_convert_fusion = (bf16[64,1280]{1,0:T(8,128)(2,1)S(1)}, bf16[64,1280]{1,0:T(8,128)(2,1)S(1)}) fusion(f32[64,1280]{1,0:T(8,128)} %param.11, f32[1280]{0:T(1024)S(1)} %convert_element_type.9, f32[64,1280]{1,0:T(8,128)} %param.13), kind=kLoop, calls=%fused_computation.8 | loop fusion | flops 327680 | bytes 988160 | tf_op jit(solution)/shard_map/convert_element_type | solution.py:130
  2.5 1.6 %collective-permute-start = (bf16[64,1280]{1,0:T(8,128)(2,1)S(1)}, bf16[64,1280]{1,0:T(8,128)(2,1)S(1)}, u32[]{:S(2)}, u32[]{:S(2)}) collective-permute-start(bf16[64,1280]{1,0:T(8,128)(2,1)S(1)} %get-tuple-element.12.refs_0_), channel_id=1, source_target_pairs={{0,4},{4,8},{8,12},{12,0},{1,5},{5,9},{9,13},{13,1},{2,6},{6,10},{... | collective-permute-start | bytes 491528 | tf_op jit(solution)/shard_map/ppermute | solution.py:15
  4.2 1.2 %collective-permute-start.3 = (bf16[64,1280]{1,0:T(8,128)(2,1)S(1)}, bf16[64,1280]{1,0:T(8,128)(2,1)S(1)}, u32[]{:S(2)}, u32[]{:S(2)}) collective-permute-start(bf16[64,1280]{1,0:T(8,128)(2,1)S(1)} %get-tuple-element.12.refs_0_), channel_id=1, source_target_pairs={{0,8},{4,12},{8,0},{12,4},{1,9},{5,13},{9,1},{13,5},{2,10},{6,14},... | collective-permute-start | bytes 491528 | tf_op jit(solution)/shard_map/ppermute | solution.py:15
  5.4 1.8 %collective-permute-start.4 = (bf16[64,1280]{1,0:T(8,128)(2,1)S(1)}, bf16[64,1280]{1,0:T(8,128)(2,1)S(1)}, u32[]{:S(2)}, u32[]{:S(2)}) collective-permute-start(bf16[64,1280]{1,0:T(8,128)(2,1)S(1)} %get-tuple-element.12.refs_0_), channel_id=1, source_target_pairs={{0,12},{4,0},{8,4},{12,8},{1,13},{5,1},{9,5},{13,9},{2,14},{6,2},{... | collective-permute-start | bytes 491528 | tf_op jit(solution)/shard_map/ppermute | solution.py:15
  7.2 0.8 fusion.3
  8.0 7.6 %collective-permute-done.refs_1_ = bf16[64,1280]{1,0:T(8,128)(2,1)S(1)} collective-permute-done((bf16[64,1280]{1,0:T(8,128)(2,1)S(1)}, bf16[64,1280]{1,0:T(8,128)(2,1)S(1)}, u32[]{:S(2)}, u32[]{:S(2)}) %collective-permute-start) | collective-permute-done | bytes 163872 | tf_op jit(solution)/shard_map/ppermute | solution.py:15
  15.6 0.0 collective-permute-start.1
  15.6 1.5 %collective-permute-start.5 = (bf16[64,1280]{1,0:T(8,128)(2,1)S(1)}, bf16[64,1280]{1,0:T(8,128)(2,1)S(1)}, u32[]{:S(2)}, u32[]{:S(2)}) collective-permute-start(bf16[64,1280]{1,0:T(8,128)(2,1)S(1)} %get-tuple-element.12.refs_0_), channel_id=1, source_target_pairs={{0,2},{1,3},{2,0},{3,1},{4,6},{5,7},{6,4},{7,5},{8,10},{9,11},{10,... | collective-permute-start | bytes 491528 | tf_op jit(solution)/shard_map/ppermute | solution.py:20
  17.0 1.8 %collective-permute-done.3.refs_2_ = bf16[64,1280]{1,0:T(8,128)(2,1)S(1)} collective-permute-done((bf16[64,1280]{1,0:T(8,128)(2,1)S(1)}, bf16[64,1280]{1,0:T(8,128)(2,1)S(1)}, u32[]{:S(2)}, u32[]{:S(2)}) %collective-permute-start.3) | collective-permute-done | bytes 163872 | tf_op jit(solution)/shard_map/ppermute | solution.py:15
  18.8 1.5 %collective-permute-start.6 = (bf16[64,1280]{1,0:T(8,128)(2,1)S(1)}, bf16[64,1280]{1,0:T(8,128)(2,1)S(1)}, u32[]{:S(2)}, u32[]{:S(2)}) collective-permute-start(bf16[64,1280]{1,0:T(8,128)(2,1)S(1)} %collective-permute-done.refs_1_), channel_id=1, source_target_pairs={{0,2},{1,3},{2,0},{3,1},{4,6},{5,7},{6,4},{7,5},{8,10},{9,11},{10,... | collective-permute-start | bytes 491528 | tf_op jit(solution)/shard_map/ppermute | solution.py:20
  20.3 0.3 collective-permute-done.4.refs_3_
  20.6 1.5 %collective-permute-start.7 = (bf16[64,1280]{1,0:T(8,128)(2,1)S(1)}, bf16[64,1280]{1,0:T(8,128)(2,1)S(1)}, u32[]{:S(2)}, u32[]{:S(2)}) collective-permute-start(bf16[64,1280]{1,0:T(8,128)(2,1)S(1)} %collective-permute-done.3.refs_2_), channel_id=1, source_target_pairs={{0,2},{1,3},{2,0},{3,1},{4,6},{5,7},{6,4},{7,5},{8,10},{9,11},{10,... | collective-permute-start | bytes 491528 | tf_op jit(solution)/shard_map/ppermute | solution.py:20
  22.1 0.0 collective-permute-done.1
  22.1 0.5 collective-permute-start.8
  22.6 0.1 pad_add_fusion.1.place_ref
  22.7 0.0 collective-permute-done.5.refs_4_
  22.7 3.4 %collective-permute-done.6.refs_5_ = bf16[64,1280]{1,0:T(8,128)(2,1)S(1)} collective-permute-done((bf16[64,1280]{1,0:T(8,128)(2,1)S(1)}, bf16[64,1280]{1,0:T(8,128)(2,1)S(1)}, u32[]{:S(2)}, u32[]{:S(2)}) %collective-permute-start.6) | collective-permute-done | bytes 163872 | tf_op jit(solution)/shard_map/ppermute | solution.py:20
  26.1 3.5 %collective-permute-done.7.refs_6_ = bf16[64,1280]{1,0:T(8,128)(2,1)S(1)} collective-permute-done((bf16[64,1280]{1,0:T(8,128)(2,1)S(1)}, bf16[64,1280]{1,0:T(8,128)(2,1)S(1)}, u32[]{:S(2)}, u32[]{:S(2)}) %collective-permute-start.7) | collective-permute-done | bytes 163872 | tf_op jit(solution)/shard_map/ppermute | solution.py:20
  29.6 3.1 %collective-permute-done.8.refs_7_ = bf16[64,1280]{1,0:T(8,128)(2,1)S(1)} collective-permute-done((bf16[64,1280]{1,0:T(8,128)(2,1)S(1)}, bf16[64,1280]{1,0:T(8,128)(2,1)S(1)}, u32[]{:S(2)}, u32[]{:S(2)}) %collective-permute-start.8) | collective-permute-done | bytes 163872 | tf_op jit(solution)/shard_map/ppermute | solution.py:20
  32.7 0.0 collective-permute-done.2.far_ref
  32.7 2.9 %copy-done = bf16[5,10,256,256]{3,2,1,0:T(8,128)(2,1)S(1)} copy-done((bf16[5,10,256,256]{3,2,1,0:T(8,128)(2,1)S(1)}, bf16[5,10,256,256]{3,2,1,0:T(8,128)(2,1)}, u32[]{:S(2)}) %copy-start) | copy-done | bytes 6553624
  35.6 9.0 %window_product.2 = (f32[64,1280]{1,0:T(8,128)S(1)}, f32[64,1280]{1,0:T(8,128)S(1)}) custom-call(s32[3,5,20]{2,1,0:T(8,128)S(1)} %pad_add_fusion.1.place_ref, bf16[5,10,256,256]{3,2,1,0:T(8,128)(2,1)S(1)} %copy-done, bf16[5,10,256,256]{3,2,1,0:T(8,128)(2,1)} %collective-permute-done.2.far_ref, bf16[64,1280]{1,0:T(8,128)(2,1)S(1)} %get-tuple-element.12.refs_0_, ...), custom_call_target="tpu_custom_call" | custom-call | flops 1677721600 | bytes 15073280 | tf_op jit(solution)/shard_map/window_product/pallas_call | solution.py:79
  44.6 1.5 %collective-permute-start.9 = (f32[64,1280]{1,0:T(8,128)S(1)}, f32[64,1280]{1,0:T(8,128)S(1)}, u32[]{:S(2)}, u32[]{:S(2)}) collective-permute-start(f32[64,1280]{1,0:T(8,128)S(1)} %get-tuple-element.15), channel_id=1, source_target_pairs={{0,2},{1,3},{2,0},{3,1},{4,6},{5,7},{6,4},{7,5},{8,10},{9,11},{10,... | collective-permute-start | bytes 983048 | tf_op jit(solution)/shard_map/ppermute | solution.py:20
  46.1 2.6 %collective-permute-start.13 = (bf16[64,1280]{1,0:T(8,128)(2,1)S(1)}, bf16[64,1280]{1,0:T(8,128)(2,1)S(1)}, u32[]{:S(2)}, u32[]{:S(2)}) collective-permute-start(bf16[64,1280]{1,0:T(8,128)(2,1)S(1)} %get-tuple-element.17.refs_0_), channel_id=1, source_target_pairs={{0,4},{4,8},{8,12},{12,0},{1,5},{5,9},{9,13},{13,1},{2,6},{6,10},{... | collective-permute-start | bytes 491528 | tf_op jit(solution)/shard_map/ppermute | solution.py:15
  48.8 0.0 collective-permute-start.14
  48.8 1.7 %collective-permute-start.15 = (bf16[64,1280]{1,0:T(8,128)(2,1)S(1)}, bf16[64,1280]{1,0:T(8,128)(2,1)S(1)}, u32[]{:S(2)}, u32[]{:S(2)}) collective-permute-start(bf16[64,1280]{1,0:T(8,128)(2,1)S(1)} %get-tuple-element.17.refs_0_), channel_id=1, source_target_pairs={{0,12},{4,0},{8,4},{12,8},{1,13},{5,1},{9,5},{13,9},{2,14},{6,2},{... | collective-permute-start | bytes 491528 | tf_op jit(solution)/shard_map/ppermute | solution.py:15
  50.5 0.5 collective-permute-start.16
  51.0 9.1 %collective-permute-done.13.refs_1_ = bf16[64,1280]{1,0:T(8,128)(2,1)S(1)} collective-permute-done((bf16[64,1280]{1,0:T(8,128)(2,1)S(1)}, bf16[64,1280]{1,0:T(8,128)(2,1)S(1)}, u32[]{:S(2)}, u32[]{:S(2)}) %collective-permute-start.13) | collective-permute-done | bytes 163872 | tf_op jit(solution)/shard_map/ppermute | solution.py:15
  60.1 0.5 collective-permute-start.17
  60.7 1.7 %collective-permute-done.14.refs_2_ = bf16[64,1280]{1,0:T(8,128)(2,1)S(1)} collective-permute-done((bf16[64,1280]{1,0:T(8,128)(2,1)S(1)}, bf16[64,1280]{1,0:T(8,128)(2,1)S(1)}, u32[]{:S(2)}, u32[]{:S(2)}) %collective-permute-start.14) | collective-permute-done | bytes 163872 | tf_op jit(solution)/shard_map/ppermute | solution.py:15
  62.4 0.5 collective-permute-start.18
  62.9 1.5 %collective-permute-start.19 = (bf16[64,1280]{1,0:T(8,128)(2,1)S(1)}, bf16[64,1280]{1,0:T(8,128)(2,1)S(1)}, u32[]{:S(2)}, u32[]{:S(2)}) collective-permute-start(bf16[64,1280]{1,0:T(8,128)(2,1)S(1)} %collective-permute-done.15.refs_3_), channel_id=1, source_target_pairs={{0,2},{1,3},{2,0},{3,1},{4,6},{5,7},{6,4},{7,5},{8,10},{9,11},{10,... | collective-permute-start | bytes 491528 | tf_op jit(solution)/shard_map/ppermute | solution.py:20
  64.4 0.3 multiply_reduce_fusion.3
  64.7 0.0 copy-start.2
  64.7 0.1 collective-permute-start.12
  64.8 0.0 collective-permute-done.16.refs_4_
  64.8 3.4 %collective-permute-start.11 = (f32[4,64]{1,0:T(4,128)S(1)}, f32[4,64]{1,0:T(4,128)S(1)}, u32[]{:S(2)}, u32[]{:S(2)}) collective-permute-start(f32[4,64]{1,0:T(4,128)S(1)} %pad_maximum_fusion), channel_id=1, source_target_pairs={{0,8},{4,12},{8,0},{12,4},{1,9},{5,13},{9,1},{13,5},{2,10},{6,14},... | collective-permute-start | bytes 3080 | tf_op jit(solution)/shard_map/ppermute | solution.py:15
  68.2 0.0 collective-permute-done.17.refs_5_
  68.2 2.8 %collective-permute-start.10 = (f32[4,64]{1,0:T(4,128)S(1)}, f32[4,64]{1,0:T(4,128)S(1)}, u32[]{:S(2)}, u32[]{:S(2)}) collective-permute-start(f32[4,64]{1,0:T(4,128)S(1)} %pad_maximum_fusion), channel_id=1, source_target_pairs={{0,4},{4,8},{8,12},{12,0},{1,5},{5,9},{9,13},{13,1},{2,6},{6,10},{... | collective-permute-start | bytes 3080 | tf_op jit(solution)/shard_map/ppermute | solution.py:15
  71.1 0.0 collective-permute-done.18.refs_6_
  71.1 1.4 %collective-permute-done.19.refs_7_ = bf16[64,1280]{1,0:T(8,128)(2,1)S(1)} collective-permute-done((bf16[64,1280]{1,0:T(8,128)(2,1)S(1)}, bf16[64,1280]{1,0:T(8,128)(2,1)S(1)}, u32[]{:S(2)}, u32[]{:S(2)}) %collective-permute-start.19) | collective-permute-done | bytes 163872 | tf_op jit(solution)/shard_map/ppermute | solution.py:20
  72.5 9.0 %window_product.3 = (f32[64,1280]{1,0:T(8,128)S(1)}, f32[64,1280]{1,0:T(8,128)S(1)}) custom-call(s32[3,5,20]{2,1,0:T(8,128)S(1)} %pad_add_fusion.1.place_ref, bf16[5,10,256,256]{3,2,1,0:T(8,128)(2,1)S(1)} %copy-done, bf16[5,10,256,256]{3,2,1,0:T(8,128)(2,1)} %collective-permute-done.2.far_ref, bf16[64,1280]{1,0:T(8,128)(2,1)S(1)} %get-tuple-element.17.refs_0_, ...), custom_call_target="tpu_custom_call" | custom-call | flops 1677721600 | bytes 15073280 | tf_op jit(solution)/shard_map/window_product/pallas_call | solution.py:79
  81.5 0.6 collective-permute-start.20
  82.1 0.0 collective-permute-done.12
  82.2 7.5 %collective-permute-done.20 = f32[64,1280]{1,0:T(8,128)S(1)} collective-permute-done((f32[64,1280]{1,0:T(8,128)S(1)}, f32[64,1280]{1,0:T(8,128)S(1)}, u32[]{:S(2)}, u32[]{:S(2)}) %collective-permute-start.20) | collective-permute-done | bytes 327712 | tf_op jit(solution)/shard_map/ppermute | solution.py:20
  89.7 1.2 %multiply_add_fusion = (f32[64,1280]{1,0:T(8,128)}, f32[64,1280]{1,0:T(8,128)}, f32[64,1280]{1,0:T(8,128)}, f32[64,1280]{1,0:T(8,128)}) fusion(f32[64,1280]{1,0:T(8,128)S(1)} %copy-done.1, f32[64]{0:T(128)S(1)} %get-tuple-element.26, f32[64,1280]{1,0:T(8,128)S(1)} %copy-done.3, f32[64,1280]{1,0:T(8,128)S(1)} %get-tuple-element.28, ...), kind=kLoop, calls=%fused_computation.1 | loop fusion | flops 819200 | bytes 3610112 | tf_op jit(solution)/shard_map/add | solution.py:176
  (18 shorter events, 0.1 us)
Async XLA Ops:
  0.6 32.1 %collective-permute-start.2 = (bf16[5,10,256,256]{3,2,1,0:T(8,128)(2,1)}, bf16[5,10,256,256]{3,2,1,0:T(8,128)(2,1)}, u32[]{:S(2)}, u32[]{:S(2)}) collective-permute-start(bf16[5,10,256,256]{3,2,1,0:T(8,128)(2,1)} %near_ref.3), channel_id=1, source_target_pairs={{0,1},{1,0},{2,3},{3,2},{4,5},{5,4},{6,7},{7,6},{8,9},{9,8},{10,11... | collective-permute-start | bytes 19660808 | tf_op jit(solution)/shard_map/ppermute | solution.py:20
  2.5 13.0 %collective-permute-start = (bf16[64,1280]{1,0:T(8,128)(2,1)S(1)}, bf16[64,1280]{1,0:T(8,128)(2,1)S(1)}, u32[]{:S(2)}, u32[]{:S(2)}) collective-permute-start(bf16[64,1280]{1,0:T(8,128)(2,1)S(1)} %get-tuple-element.12.refs_0_), channel_id=1, source_target_pairs={{0,4},{4,8},{8,12},{12,0},{1,5},{5,9},{9,13},{13,1},{2,6},{6,10},{... | collective-permute-start | bytes 491528 | tf_op jit(solution)/shard_map/ppermute | solution.py:15
  4.2 14.6 %collective-permute-start.3 = (bf16[64,1280]{1,0:T(8,128)(2,1)S(1)}, bf16[64,1280]{1,0:T(8,128)(2,1)S(1)}, u32[]{:S(2)}, u32[]{:S(2)}) collective-permute-start(bf16[64,1280]{1,0:T(8,128)(2,1)S(1)} %get-tuple-element.12.refs_0_), channel_id=1, source_target_pairs={{0,8},{4,12},{8,0},{12,4},{1,9},{5,13},{9,1},{13,5},{2,10},{6,14},... | collective-permute-start | bytes 491528 | tf_op jit(solution)/shard_map/ppermute | solution.py:15
  5.4 15.2 %collective-permute-start.4 = (bf16[64,1280]{1,0:T(8,128)(2,1)S(1)}, bf16[64,1280]{1,0:T(8,128)(2,1)S(1)}, u32[]{:S(2)}, u32[]{:S(2)}) collective-permute-start(bf16[64,1280]{1,0:T(8,128)(2,1)S(1)} %get-tuple-element.12.refs_0_), channel_id=1, source_target_pairs={{0,12},{4,0},{8,4},{12,8},{1,13},{5,1},{9,5},{13,9},{2,14},{6,2},{... | collective-permute-start | bytes 491528 | tf_op jit(solution)/shard_map/ppermute | solution.py:15
  15.6 6.5 %collective-permute-start.1 = (s32[3,5,10]{2,1,0:T(8,128)S(1)}, s32[3,5,10]{2,1,0:T(8,128)S(1)}, u32[]{:S(2)}, u32[]{:S(2)}) collective-permute-start(s32[3,5,10]{2,1,0:T(8,128)S(1)} %pad_add_fusion), channel_id=1, source_target_pairs={{0,1},{1,0},{2,3},{3,2},{4,5},{5,4},{6,7},{7,6},{8,9},{9,8},{10,11... | collective-permute-start | bytes 1808 | tf_op jit(solution)/shard_map/ppermute | solution.py:20
  15.6 7.1 %collective-permute-start.5 = (bf16[64,1280]{1,0:T(8,128)(2,1)S(1)}, bf16[64,1280]{1,0:T(8,128)(2,1)S(1)}, u32[]{:S(2)}, u32[]{:S(2)}) collective-permute-start(bf16[64,1280]{1,0:T(8,128)(2,1)S(1)} %get-tuple-element.12.refs_0_), channel_id=1, source_target_pairs={{0,2},{1,3},{2,0},{3,1},{4,6},{5,7},{6,4},{7,5},{8,10},{9,11},{10,... | collective-permute-start | bytes 491528 | tf_op jit(solution)/shard_map/ppermute | solution.py:20
  18.8 7.3 %collective-permute-start.6 = (bf16[64,1280]{1,0:T(8,128)(2,1)S(1)}, bf16[64,1280]{1,0:T(8,128)(2,1)S(1)}, u32[]{:S(2)}, u32[]{:S(2)}) collective-permute-start(bf16[64,1280]{1,0:T(8,128)(2,1)S(1)} %collective-permute-done.refs_1_), channel_id=1, source_target_pairs={{0,2},{1,3},{2,0},{3,1},{4,6},{5,7},{6,4},{7,5},{8,10},{9,11},{10,... | collective-permute-start | bytes 491528 | tf_op jit(solution)/shard_map/ppermute | solution.py:20
  20.6 9.0 %collective-permute-start.7 = (bf16[64,1280]{1,0:T(8,128)(2,1)S(1)}, bf16[64,1280]{1,0:T(8,128)(2,1)S(1)}, u32[]{:S(2)}, u32[]{:S(2)}) collective-permute-start(bf16[64,1280]{1,0:T(8,128)(2,1)S(1)} %collective-permute-done.3.refs_2_), channel_id=1, source_target_pairs={{0,2},{1,3},{2,0},{3,1},{4,6},{5,7},{6,4},{7,5},{8,10},{9,11},{10,... | collective-permute-start | bytes 491528 | tf_op jit(solution)/shard_map/ppermute | solution.py:20
  22.1 10.6 %collective-permute-start.8 = (bf16[64,1280]{1,0:T(8,128)(2,1)S(1)}, bf16[64,1280]{1,0:T(8,128)(2,1)S(1)}, u32[]{:S(2)}, u32[]{:S(2)}) collective-permute-start(bf16[64,1280]{1,0:T(8,128)(2,1)S(1)} %collective-permute-done.4.refs_3_), channel_id=1, source_target_pairs={{0,2},{1,3},{2,0},{3,1},{4,6},{5,7},{6,4},{7,5},{8,10},{9,11},{10,... | collective-permute-start | bytes 491528 | tf_op jit(solution)/shard_map/ppermute | solution.py:20
  22.6 27.9 %copy-start.4 = (s32[1280]{0:T(1024)S(1)}, s32[1280]{0:T(1024)}, u32[]{:S(2)}) copy-start(s32[1280]{0:T(1024)} %param.10) | copy-start | bytes 15364
  32.7 2.9 %copy-start = (bf16[5,10,256,256]{3,2,1,0:T(8,128)(2,1)S(1)}, bf16[5,10,256,256]{3,2,1,0:T(8,128)(2,1)}, u32[]{:S(2)}) copy-start(bf16[5,10,256,256]{3,2,1,0:T(8,128)(2,1)} %near_ref.3) | copy-start | bytes 19660804
  35.6 28.8 %copy-start.1 = (f32[64,1280]{1,0:T(8,128)S(1)}, f32[64,1280]{1,0:T(8,128)}, u32[]{:S(2)}) copy-start(f32[64,1280]{1,0:T(8,128)} %param.13) | copy-start | bytes 983044
  35.6 28.8 %copy-start.3 = (f32[64,1280]{1,0:T(8,128)S(1)}, f32[64,1280]{1,0:T(8,128)}, u32[]{:S(2)}) copy-start(f32[64,1280]{1,0:T(8,128)} %param.12) | copy-start | bytes 983044
  44.6 19.8 %collective-permute-start.9 = (f32[64,1280]{1,0:T(8,128)S(1)}, f32[64,1280]{1,0:T(8,128)S(1)}, u32[]{:S(2)}, u32[]{:S(2)}) collective-permute-start(f32[64,1280]{1,0:T(8,128)S(1)} %get-tuple-element.15), channel_id=1, source_target_pairs={{0,2},{1,3},{2,0},{3,1},{4,6},{5,7},{6,4},{7,5},{8,10},{9,11},{10,... | collective-permute-start | bytes 983048 | tf_op jit(solution)/shard_map/ppermute | solution.py:20
  46.1 14.0 %collective-permute-start.13 = (bf16[64,1280]{1,0:T(8,128)(2,1)S(1)}, bf16[64,1280]{1,0:T(8,128)(2,1)S(1)}, u32[]{:S(2)}, u32[]{:S(2)}) collective-permute-start(bf16[64,1280]{1,0:T(8,128)(2,1)S(1)} %get-tuple-element.17.refs_0_), channel_id=1, source_target_pairs={{0,4},{4,8},{8,12},{12,0},{1,5},{5,9},{9,13},{13,1},{2,6},{6,10},{... | collective-permute-start | bytes 491528 | tf_op jit(solution)/shard_map/ppermute | solution.py:15
  48.8 13.6 %collective-permute-start.14 = (bf16[64,1280]{1,0:T(8,128)(2,1)S(1)}, bf16[64,1280]{1,0:T(8,128)(2,1)S(1)}, u32[]{:S(2)}, u32[]{:S(2)}) collective-permute-start(bf16[64,1280]{1,0:T(8,128)(2,1)S(1)} %get-tuple-element.17.refs_0_), channel_id=1, source_target_pairs={{0,8},{4,12},{8,0},{12,4},{1,9},{5,13},{9,1},{13,5},{2,10},{6,14},... | collective-permute-start | bytes 491528 | tf_op jit(solution)/shard_map/ppermute | solution.py:15
  48.8 14.1 %collective-permute-start.15 = (bf16[64,1280]{1,0:T(8,128)(2,1)S(1)}, bf16[64,1280]{1,0:T(8,128)(2,1)S(1)}, u32[]{:S(2)}, u32[]{:S(2)}) collective-permute-start(bf16[64,1280]{1,0:T(8,128)(2,1)S(1)} %get-tuple-element.17.refs_0_), channel_id=1, source_target_pairs={{0,12},{4,0},{8,4},{12,8},{1,13},{5,1},{9,5},{13,9},{2,14},{6,2},{... | collective-permute-start | bytes 491528 | tf_op jit(solution)/shard_map/ppermute | solution.py:15
  50.5 14.3 %collective-permute-start.16 = (bf16[64,1280]{1,0:T(8,128)(2,1)S(1)}, bf16[64,1280]{1,0:T(8,128)(2,1)S(1)}, u32[]{:S(2)}, u32[]{:S(2)}) collective-permute-start(bf16[64,1280]{1,0:T(8,128)(2,1)S(1)} %get-tuple-element.17.refs_0_), channel_id=1, source_target_pairs={{0,2},{1,3},{2,0},{3,1},{4,6},{5,7},{6,4},{7,5},{8,10},{9,11},{10,... | collective-permute-start | bytes 491528 | tf_op jit(solution)/shard_map/ppermute | solution.py:20
  60.1 8.1 %collective-permute-start.17 = (bf16[64,1280]{1,0:T(8,128)(2,1)S(1)}, bf16[64,1280]{1,0:T(8,128)(2,1)S(1)}, u32[]{:S(2)}, u32[]{:S(2)}) collective-permute-start(bf16[64,1280]{1,0:T(8,128)(2,1)S(1)} %collective-permute-done.13.refs_1_), channel_id=1, source_target_pairs={{0,2},{1,3},{2,0},{3,1},{4,6},{5,7},{6,4},{7,5},{8,10},{9,11},{10,... | collective-permute-start | bytes 491528 | tf_op jit(solution)/shard_map/ppermute | solution.py:20
  62.4 8.7 %collective-permute-start.18 = (bf16[64,1280]{1,0:T(8,128)(2,1)S(1)}, bf16[64,1280]{1,0:T(8,128)(2,1)S(1)}, u32[]{:S(2)}, u32[]{:S(2)}) collective-permute-start(bf16[64,1280]{1,0:T(8,128)(2,1)S(1)} %collective-permute-done.14.refs_2_), channel_id=1, source_target_pairs={{0,2},{1,3},{2,0},{3,1},{4,6},{5,7},{6,4},{7,5},{8,10},{9,11},{10,... | collective-permute-start | bytes 491528 | tf_op jit(solution)/shard_map/ppermute | solution.py:20
  62.9 9.6 %collective-permute-start.19 = (bf16[64,1280]{1,0:T(8,128)(2,1)S(1)}, bf16[64,1280]{1,0:T(8,128)(2,1)S(1)}, u32[]{:S(2)}, u32[]{:S(2)}) collective-permute-start(bf16[64,1280]{1,0:T(8,128)(2,1)S(1)} %collective-permute-done.15.refs_3_), channel_id=1, source_target_pairs={{0,2},{1,3},{2,0},{3,1},{4,6},{5,7},{6,4},{7,5},{8,10},{9,11},{10,... | collective-permute-start | bytes 491528 | tf_op jit(solution)/shard_map/ppermute | solution.py:20
  64.7 25.0 %copy-start.2 = (f32[64,1280]{1,0:T(8,128)S(1)}, f32[64,1280]{1,0:T(8,128)}, u32[]{:S(2)}) copy-start(f32[64,1280]{1,0:T(8,128)} %param.11) | copy-start | bytes 983044
  64.7 17.4 %collective-permute-start.12 = (f32[4,64]{1,0:T(4,128)S(1)}, f32[4,64]{1,0:T(4,128)S(1)}, u32[]{:S(2)}, u32[]{:S(2)}) collective-permute-start(f32[4,64]{1,0:T(4,128)S(1)} %pad_maximum_fusion), channel_id=1, source_target_pairs={{0,12},{4,0},{8,4},{12,8},{1,13},{5,1},{9,5},{13,9},{2,14},{6,2},{... | collective-permute-start | bytes 3080 | tf_op jit(solution)/shard_map/ppermute | solution.py:15
  64.8 17.4 %collective-permute-start.11 = (f32[4,64]{1,0:T(4,128)S(1)}, f32[4,64]{1,0:T(4,128)S(1)}, u32[]{:S(2)}, u32[]{:S(2)}) collective-permute-start(f32[4,64]{1,0:T(4,128)S(1)} %pad_maximum_fusion), channel_id=1, source_target_pairs={{0,8},{4,12},{8,0},{12,4},{1,9},{5,13},{9,1},{13,5},{2,10},{6,14},... | collective-permute-start | bytes 3080 | tf_op jit(solution)/shard_map/ppermute | solution.py:15
  68.2 13.9 %collective-permute-start.10 = (f32[4,64]{1,0:T(4,128)S(1)}, f32[4,64]{1,0:T(4,128)S(1)}, u32[]{:S(2)}, u32[]{:S(2)}) collective-permute-start(f32[4,64]{1,0:T(4,128)S(1)} %pad_maximum_fusion), channel_id=1, source_target_pairs={{0,4},{4,8},{8,12},{12,0},{1,5},{5,9},{9,13},{13,1},{2,6},{6,10},{... | collective-permute-start | bytes 3080 | tf_op jit(solution)/shard_map/ppermute | solution.py:15
  81.5 8.1 %collective-permute-start.20 = (f32[64,1280]{1,0:T(8,128)S(1)}, f32[64,1280]{1,0:T(8,128)S(1)}, u32[]{:S(2)}, u32[]{:S(2)}) collective-permute-start(f32[64,1280]{1,0:T(8,128)S(1)} %get-tuple-element.19), channel_id=1, source_target_pairs={{0,2},{1,3},{2,0},{3,1},{4,6},{5,7},{6,4},{7,5},{8,10},{9,11},{10,... | collective-permute-start | bytes 983048 | tf_op jit(solution)/shard_map/ppermute | solution.py:20
